TPU v7x, 32 devices: a whole 2x2x4 slice. The times are simulated.
32 devices in a mesh: rows: 32 (over z, y, x, core).
Axes of the slice: x: 2, y: 2, z: 4, core: 2. Of those that a mesh axis runs over, the one named last changes fastest.
Arguments:
- right_sides: float32 [65536, 512], P('rows'), may hold values from -6 to 6
- leaf_inverse: float32 [65536, 512], P('rows'), may hold values from -3 to 3, as said below
- mid_proj: float32 [65536, 256], P('rows'), may hold values from -0.046875 to 0.046875
- mid_basis: float32 [65536, 256], P('rows'), may hold values from -0.375 to 0.375
- mid_cap: float32 [2, 512, 512], replicated, may hold values from -3 to 3, as said below
- top_proj: float32 [65536, 256], P('rows'), may hold values from -0.03125 to 0.03125
- top_basis: float32 [65536, 256], P('rows'), may hold values from -0.375 to 0.375
- top_cap: float32 [1, 512, 512], replicated, may hold values from -3 to 3, as said below
Outputs:
- solution: float32 [65536, 512], P('rows')
Inputs may be any that keep to these rules, and one draw needn't show every extreme that they name: `leaf_inverse`: each row's entry at its own position within its block is the largest. `mid_cap`: each row's diagonal entry is its largest. `top_cap`: each row's diagonal entry is its largest.
All inputs are finite; a program needn't handle non-finite values.
Results may differ from a plain program's by a relative error of at most 0.00014.
Values sent between devices are 32-bit elements; how exact they have to be, the bound alone decides.
A program may use at most 128 MiB of HBM per device.

v0:
```python
import jax
import jax.numpy as jnp
from jax import lax
from jax.sharding import PartitionSpec as P

PRECISE = lax.Precision.HIGHEST


def partner(value, axis, distance):
    mask = 2**distance
    pairs = [(source, source ^ mask) for source in range(lax.axis_size(axis))]
    return lax.ppermute(value, axis, pairs)


def leaf_apply(leaf_inverse, right_sides):
    order = leaf_inverse.shape[1]
    block_count = right_sides.shape[0] // order
    blocks = leaf_inverse.reshape(block_count, order, order)
    pieces = right_sides.reshape(block_count, order, right_sides.shape[1])
    return jnp.einsum("bij,bjr->bir", blocks, pieces, precision=PRECISE).reshape(right_sides.shape)


def project(factor, field):
    return jnp.einsum("nk,nr->kr", factor, field, precision=PRECISE)


def group_sum(projection, first_bit, levels):
    for bit_no in range(first_bit, levels):
        projection = projection + partner(projection, "rows", bit_no)
    return projection


def couple(projection, capacity, bit_no):
    sibling_proj = partner(projection, "rows", bit_no)
    position = lax.axis_index("rows")
    upper_half = position >> bit_no & 1
    pair_no = position >> bit_no + 1
    rank_size = projection.shape[0]
    matrix = lax.dynamic_index_in_dim(capacity, pair_no, 0, keepdims=False)
    cap_rows = lax.dynamic_slice_in_dim(matrix, upper_half * rank_size, rank_size, 0)
    leading = jnp.where(upper_half == 0, sibling_proj, projection)
    trailing = jnp.where(upper_half == 0, projection, sibling_proj)
    return jnp.dot(cap_rows[:, :rank_size], leading, precision=PRECISE) + jnp.dot(
        cap_rows[:, rank_size:], trailing, precision=PRECISE
    )


def per_device(
    right_sides, leaf_inverse, mid_proj, mid_basis, mid_cap, top_proj, top_basis, top_cap
):
    levels = lax.axis_size("rows").bit_length() - 1
    leaf_out = leaf_apply(leaf_inverse, right_sides)
    coef_mid = couple(group_sum(project(mid_proj, leaf_out), 0, levels - 2), mid_cap, levels - 2)
    mid_field = leaf_out - jnp.dot(mid_basis, coef_mid, precision=PRECISE)
    coef_top = couple(group_sum(project(top_proj, mid_field), 0, levels - 1), top_cap, levels - 1)
    return mid_field - jnp.dot(top_basis, coef_top, precision=PRECISE)


def solution(mesh):
    placed = (
        P("rows", None),
        P("rows", None),
        P("rows", None),
        P("rows", None),
        P(),
        P("rows", None),
        P("rows", None),
        P(),
    )
    return jax.shard_map(
        per_device, mesh=mesh, in_specs=placed, out_specs=P("rows", None), check_vma=False
    )
```

profile of v0, /device:TPU:0, one launch (start us, length us, event | category | flops | bytes accessed | tf_op | source)
XLA Modules:
  0.0 153.9 jit_solution(14851921347995096125)
XLA Ops:
  0.0 9.4 %fusion.14 = f32[4,512,512]{2,1,0:T(8,128)S(1)} fusion(f32[4,512,512]{2,1,0:T(8,128)} %bitcast.27, f32[4,512,512]{2,1,0:T(8,128)} %bitcast.28), kind=kOutput, calls=%fused_computation.22 | convolution fusion | flops 6442450944 | bytes 12582912 | tf_op jit(solution)/shard_map/bij,bjr->bir/dot_general | solution.py:20
  9.5 6.7 %convolution_bitcast_fusion.1 = f32[256,512]{0,1:T(8,128)S(1)} fusion(f32[2048,512]{1,0:T(8,128)S(1)} %bitcast.25, f32[2048,256]{1,0:T(8,128)S(1)} %copy-done.5), kind=kOutput, calls=%fused_computation.3 | convolution fusion | flops 3221225472 | bytes 6815744 | tf_op jit(solution)/shard_map/nk,nr->kr/dot_general | solution.py:24
  16.1 0.5 collective-permute-start
  16.7 1.5 collective-permute-done
  18.3 2.9 %collective-permute-start.1 = (f32[256,512]{0,1:T(8,128)S(1)}, f32[256,512]{0,1:T(8,128)S(1)}, u32[]{:S(2)}, u32[]{:S(2)}) collective-permute-start(f32[256,512]{0,1:T(8,128)S(1)} %add.44), channel_id=1, source_target_pairs={{0,2},{1,3},{2,0},{3,1},{4,6},{5,7},{6,4},{7,5},{8,10},{9,11},{10,... | collective-permute-start | bytes 1572872 | tf_op jit(solution)/shard_map/ppermute | solution.py:12
  21.2 12.2 %collective-permute-done.1 = f32[256,512]{0,1:T(8,128)S(1)} collective-permute-done((f32[256,512]{0,1:T(8,128)S(1)}, f32[256,512]{0,1:T(8,128)S(1)}, u32[]{:S(2)}, u32[]{:S(2)}) %collective-permute-start.1) | collective-permute-done | bytes 524320 | tf_op jit(solution)/shard_map/ppermute | solution.py:12
  33.5 1.8 %collective-permute-start.2 = (f32[256,512]{0,1:T(8,128)S(1)}, f32[256,512]{0,1:T(8,128)S(1)}, u32[]{:S(2)}, u32[]{:S(2)}) collective-permute-start(f32[256,512]{0,1:T(8,128)S(1)} %add.45), channel_id=1, source_target_pairs={{0,4},{1,5},{2,6},{3,7},{4,0},{5,1},{6,2},{7,3},{8,12},{9,13},{10,... | collective-permute-start | bytes 1572872 | tf_op jit(solution)/shard_map/ppermute | solution.py:12
  35.3 11.7 %collective-permute-done.2 = f32[256,512]{0,1:T(8,128)S(1)} collective-permute-done((f32[256,512]{0,1:T(8,128)S(1)}, f32[256,512]{0,1:T(8,128)S(1)}, u32[]{:S(2)}, u32[]{:S(2)}) %collective-permute-start.2) | collective-permute-done | bytes 524320 | tf_op jit(solution)/shard_map/ppermute | solution.py:12
  47.1 1.6 %collective-permute-start.3 = (f32[256,512]{0,1:T(8,128)S(1)}, f32[256,512]{0,1:T(8,128)S(1)}, u32[]{:S(2)}, u32[]{:S(2)}) collective-permute-start(f32[256,512]{0,1:T(8,128)S(1)} %add.46), channel_id=1, source_target_pairs={{0,8},{1,9},{2,10},{3,11},{4,12},{5,13},{6,14},{7,15},{8,0},{9,1},... | collective-permute-start | bytes 1572872 | tf_op jit(solution)/shard_map/ppermute | solution.py:12
  48.7 5.4 %copy.9 = f32[2048,512]{0,1:T(8,128)} copy(f32[2048,512]{1,0:T(8,128)} %bitcast.26) | data formatting | bytes 8388608 | tf_op jit(solution)/shard_map/reshape | solution.py:20
  54.1 1.3 dynamic-slice_bitcast_fusion.1
  55.3 4.4 %collective-permute-done.3 = f32[256,512]{0,1:T(8,128)S(1)} collective-permute-done((f32[256,512]{0,1:T(8,128)S(1)}, f32[256,512]{0,1:T(8,128)S(1)}, u32[]{:S(2)}, u32[]{:S(2)}) %collective-permute-start.3) | collective-permute-done | bytes 524320 | tf_op jit(solution)/shard_map/ppermute | solution.py:12
  59.7 0.6 fusion.3
  60.4 0.6 convolution_add_fusion.1
  61.1 7.0 %bitcast_subtract_fusion.1 = f32[2048,512]{0,1:T(8,128)S(1)} fusion(f32[2048,512]{0,1:T(8,128)S(1)} %copy-done.4, f32[256,512]{1,0:T(8,128)S(1)} %convolution_add_fusion.1, f32[2048,256]{1,0:T(8,128)S(1)} %copy-done), kind=kOutput, calls=%fused_computation.1 | convolution fusion | flops 3222274048 | bytes 11010048 | tf_op jit(solution)/shard_map/dot_general | solution.py:54
  68.1 3.4 %convolution_bitcast_fusion = f32[256,512]{0,1:T(8,128)S(1)} fusion(f32[2048,512]{0,1:T(8,128)S(1)} %bitcast_subtract_fusion.1, f32[2048,256]{1,0:T(8,128)S(1)} %copy-done.6), kind=kOutput, calls=%fused_computation.2 | convolution fusion | flops 3221225472 | bytes 6815744 | tf_op jit(solution)/shard_map/nk,nr->kr/dot_general | solution.py:24
  71.6 0.1 collective-permute-start.4
  71.7 1.9 %collective-permute-done.4 = f32[256,512]{0,1:T(8,128)S(1)} collective-permute-done((f32[256,512]{0,1:T(8,128)S(1)}, f32[256,512]{0,1:T(8,128)S(1)}, u32[]{:S(2)}, u32[]{:S(2)}) %collective-permute-start.4) | collective-permute-done | bytes 524320 | tf_op jit(solution)/shard_map/ppermute | solution.py:12
  73.6 1.1 collective-permute-start.5
  74.8 12.9 %collective-permute-done.5 = f32[256,512]{0,1:T(8,128)S(1)} collective-permute-done((f32[256,512]{0,1:T(8,128)S(1)}, f32[256,512]{0,1:T(8,128)S(1)}, u32[]{:S(2)}, u32[]{:S(2)}) %collective-permute-start.5) | collective-permute-done | bytes 524320 | tf_op jit(solution)/shard_map/ppermute | solution.py:12
  87.7 1.4 collective-permute-start.6
  89.1 12.0 %collective-permute-done.6 = f32[256,512]{0,1:T(8,128)S(1)} collective-permute-done((f32[256,512]{0,1:T(8,128)S(1)}, f32[256,512]{0,1:T(8,128)S(1)}, u32[]{:S(2)}, u32[]{:S(2)}) %collective-permute-start.6) | collective-permute-done | bytes 524320 | tf_op jit(solution)/shard_map/ppermute | solution.py:12
  101.2 0.1 add.51
  101.2 1.2 collective-permute-start.7
  102.5 11.1 %collective-permute-done.7 = f32[256,512]{0,1:T(8,128)S(1)} collective-permute-done((f32[256,512]{0,1:T(8,128)S(1)}, f32[256,512]{0,1:T(8,128)S(1)}, u32[]{:S(2)}, u32[]{:S(2)}) %collective-permute-start.7) | collective-permute-done | bytes 524320 | tf_op jit(solution)/shard_map/ppermute | solution.py:12
  113.6 2.2 %collective-permute-start.8 = (f32[256,512]{0,1:T(8,128)S(1)}, f32[256,512]{0,1:T(8,128)S(1)}, u32[]{:S(2)}, u32[]{:S(2)}) collective-permute-start(f32[256,512]{0,1:T(8,128)S(1)} %add.52), channel_id=1, source_target_pairs={{0,16},{1,17},{2,18},{3,19},{4,20},{5,21},{6,22},{7,23},{8,24},{9,... | collective-permute-start | bytes 1572872 | tf_op jit(solution)/shard_map/ppermute | solution.py:12
  115.8 1.2 dynamic-slice_bitcast_fusion
  117.1 20.0 %collective-permute-done.8 = f32[256,512]{0,1:T(8,128)S(1)} collective-permute-done((f32[256,512]{0,1:T(8,128)S(1)}, f32[256,512]{0,1:T(8,128)S(1)}, u32[]{:S(2)}, u32[]{:S(2)}) %collective-permute-start.8) | collective-permute-done | bytes 524320 | tf_op jit(solution)/shard_map/ppermute | solution.py:12
  137.1 0.6 fusion
  137.7 0.6 convolution_add_fusion
  138.4 10.2 %bitcast_subtract_fusion = f32[2048,512]{0,1:T(8,128)} fusion(f32[2048,512]{0,1:T(8,128)S(1)} %copy-done.3, f32[256,512]{1,0:T(8,128)S(1)} %convolution_add_fusion, f32[2048,256]{1,0:T(8,128)} %param.14), kind=kOutput, calls=%fused_computation | convolution fusion | flops 3222274048 | bytes 11010048 | tf_op jit(solution)/shard_map/dot_general | solution.py:56
  148.6 5.3 %copy.10 = f32[2048,512]{1,0:T(8,128)} copy(f32[2048,512]{0,1:T(8,128)} %bitcast_subtract_fusion) | data formatting | bytes 8388608 | tf_op jit(solution)/shard_map/sub | solution.py:56
  (20 shorter events, 0.4 us)
Async XLA Ops:
  0.0 61.0 %copy-start = (f32[2048,256]{1,0:T(8,128)S(1)}, f32[2048,256]{1,0:T(8,128)}, u32[]{:S(2)}) copy-start(f32[2048,256]{1,0:T(8,128)} %param.11) | copy-start | bytes 6291460
  0.0 9.5 %copy-start.5 = (f32[2048,256]{1,0:T(8,128)S(1)}, f32[2048,256]{1,0:T(8,128)}, u32[]{:S(2)}) copy-start(f32[2048,256]{1,0:T(8,128)} %param.10) | copy-start | bytes 6291460
  9.4 8.8 %copy-start.1 = (f32[4,512,512]{2,1,0:T(8,128)}, f32[4,512,512]{2,1,0:T(8,128)S(1)}, u32[]{:S(2)}) copy-start(f32[4,512,512]{2,1,0:T(8,128)S(1)} %fusion.14) | copy-start | bytes 12582916
  16.1 2.1 %collective-permute-start = (f32[256,512]{0,1:T(8,128)S(1)}, f32[256,512]{0,1:T(8,128)S(1)}, u32[]{:S(2)}, u32[]{:S(2)}) collective-permute-start(f32[256,512]{0,1:T(8,128)S(1)} %convolution_bitcast_fusion.1), channel_id=1, source_target_pairs={{0,1},{1,0},{2,3},{3,2},{4,5},{5,4},{6,7},{7,6},{8,9},{9,8},{10,11... | collective-permute-start | bytes 1572872 | tf_op jit(solution)/shard_map/ppermute | solution.py:12
  18.3 15.2 %collective-permute-start.1 = (f32[256,512]{0,1:T(8,128)S(1)}, f32[256,512]{0,1:T(8,128)S(1)}, u32[]{:S(2)}, u32[]{:S(2)}) collective-permute-start(f32[256,512]{0,1:T(8,128)S(1)} %add.44), channel_id=1, source_target_pairs={{0,2},{1,3},{2,0},{3,1},{4,6},{5,7},{6,4},{7,5},{8,10},{9,11},{10,... | collective-permute-start | bytes 1572872 | tf_op jit(solution)/shard_map/ppermute | solution.py:12
  33.5 13.5 %collective-permute-start.2 = (f32[256,512]{0,1:T(8,128)S(1)}, f32[256,512]{0,1:T(8,128)S(1)}, u32[]{:S(2)}, u32[]{:S(2)}) collective-permute-start(f32[256,512]{0,1:T(8,128)S(1)} %add.45), channel_id=1, source_target_pairs={{0,4},{1,5},{2,6},{3,7},{4,0},{5,1},{6,2},{7,3},{8,12},{9,13},{10,... | collective-permute-start | bytes 1572872 | tf_op jit(solution)/shard_map/ppermute | solution.py:12
  47.1 12.6 %collective-permute-start.3 = (f32[256,512]{0,1:T(8,128)S(1)}, f32[256,512]{0,1:T(8,128)S(1)}, u32[]{:S(2)}, u32[]{:S(2)}) collective-permute-start(f32[256,512]{0,1:T(8,128)S(1)} %add.46), channel_id=1, source_target_pairs={{0,8},{1,9},{2,10},{3,11},{4,12},{5,13},{6,14},{7,15},{8,0},{9,1},... | collective-permute-start | bytes 1572872 | tf_op jit(solution)/shard_map/ppermute | solution.py:12
  54.0 7.0 %copy-start.4 = (f32[2048,512]{0,1:T(8,128)S(1)}, f32[2048,512]{0,1:T(8,128)}, u32[]{:S(2)}) copy-start(f32[2048,512]{0,1:T(8,128)} %copy.9) | copy-start | bytes 12582916
  61.0 7.1 %copy-start.6 = (f32[2048,256]{1,0:T(8,128)S(1)}, f32[2048,256]{1,0:T(8,128)}, u32[]{:S(2)}) copy-start(f32[2048,256]{1,0:T(8,128)} %param.13) | copy-start | bytes 6291460
  68.1 19.6 %copy-start.2 = (f32[2048,512]{0,1:T(8,128)}, f32[2048,512]{0,1:T(8,128)S(1)}, u32[]{:S(2)}) copy-start(f32[2048,512]{0,1:T(8,128)S(1)} %bitcast_subtract_fusion.1) | copy-start | bytes 12582916
  71.6 2.0 %collective-permute-start.4 = (f32[256,512]{0,1:T(8,128)S(1)}, f32[256,512]{0,1:T(8,128)S(1)}, u32[]{:S(2)}, u32[]{:S(2)}) collective-permute-start(f32[256,512]{0,1:T(8,128)S(1)} %convolution_bitcast_fusion), channel_id=1, source_target_pairs={{0,1},{1,0},{2,3},{3,2},{4,5},{5,4},{6,7},{7,6},{8,9},{9,8},{10,11... | collective-permute-start | bytes 1572872 | tf_op jit(solution)/shard_map/ppermute | solution.py:12
  73.6 14.0 %collective-permute-start.5 = (f32[256,512]{0,1:T(8,128)S(1)}, f32[256,512]{0,1:T(8,128)S(1)}, u32[]{:S(2)}, u32[]{:S(2)}) collective-permute-start(f32[256,512]{0,1:T(8,128)S(1)} %add.49), channel_id=1, source_target_pairs={{0,2},{1,3},{2,0},{3,1},{4,6},{5,7},{6,4},{7,5},{8,10},{9,11},{10,... | collective-permute-start | bytes 1572872 | tf_op jit(solution)/shard_map/ppermute | solution.py:12
  87.7 13.4 %collective-permute-start.6 = (f32[256,512]{0,1:T(8,128)S(1)}, f32[256,512]{0,1:T(8,128)S(1)}, u32[]{:S(2)}, u32[]{:S(2)}) collective-permute-start(f32[256,512]{0,1:T(8,128)S(1)} %add.50), channel_id=1, source_target_pairs={{0,4},{1,5},{2,6},{3,7},{4,0},{5,1},{6,2},{7,3},{8,12},{9,13},{10,... | collective-permute-start | bytes 1572872 | tf_op jit(solution)/shard_map/ppermute | solution.py:12
  101.2 12.3 %collective-permute-start.7 = (f32[256,512]{0,1:T(8,128)S(1)}, f32[256,512]{0,1:T(8,128)S(1)}, u32[]{:S(2)}, u32[]{:S(2)}) collective-permute-start(f32[256,512]{0,1:T(8,128)S(1)} %add.51), channel_id=1, source_target_pairs={{0,8},{1,9},{2,10},{3,11},{4,12},{5,13},{6,14},{7,15},{8,0},{9,1},... | collective-permute-start | bytes 1572872 | tf_op jit(solution)/shard_map/ppermute | solution.py:12
  113.6 23.5 %collective-permute-start.8 = (f32[256,512]{0,1:T(8,128)S(1)}, f32[256,512]{0,1:T(8,128)S(1)}, u32[]{:S(2)}, u32[]{:S(2)}) collective-permute-start(f32[256,512]{0,1:T(8,128)S(1)} %add.52), channel_id=1, source_target_pairs={{0,16},{1,17},{2,18},{3,19},{4,20},{5,21},{6,22},{7,23},{8,24},{9,... | collective-permute-start | bytes 1572872 | tf_op jit(solution)/shard_map/ppermute | solution.py:12
  115.8 22.5 %copy-start.3 = (f32[2048,512]{0,1:T(8,128)S(1)}, f32[2048,512]{0,1:T(8,128)}, u32[]{:S(2)}) copy-start(f32[2048,512]{0,1:T(8,128)} %copy-done.2) | copy-start | bytes 12582916
where the time goes:
time: 154 us
  waiting for transfers between devices  87.7 us (57%)
  matrix products  39.3 us (26%)
  local copies, waits for them, and re-layouts  13.2 us (9%)
  starting transfers between devices  12.9 us (8%)
    ppermute x9, waiting for transfers between devices, partner(): return lax.ppermute(value, axis, pairs)  87.7 us
    ppermute x9, starting transfers between devices, partner(): return lax.ppermute(value, axis, pairs)  12.9 us
    dot_general x1, matrix products, per_device(): return mid_field - jnp.dot(top_basis, coef_top, precision=PRECISE)  10.2 us
    dot_general x2, matrix products, project(): return jnp.einsum('nk,nr->kr', factor, field, precision=PRECISE)  10.1 us
    dot_general x1, matrix products, leaf_apply(): jnp.einsum('bij,bjr->bir', blocks, pieces, precision=PRECISE)  9.43 us
    dot_general x1, matrix products, per_device(): mid_field = leaf_out - jnp.dot(mid_basis, coef_mid, precision=PRECISE)  7.04 us
    reshape x1, local copies, waits for them, and re-layouts, leaf_apply(): jnp.einsum('bij,bjr->bir', blocks, pieces, precision=PRECISE)  5.37 us
    sub x1, local copies, waits for them, and re-layouts, per_device(): return mid_field - jnp.dot(top_basis, coef_top, precision=PRECISE)  5.34 us
  transfers between devices with their start and end apart: 9, of which 9 were waited for; matrix products, arithmetic and copies ran while one was open for 5% of the time, Pallas kernels for 0%

commit v1 on v0

v1 whole, which is shorter than its diff:
```python
import functools

import jax
import jax.numpy as jnp
from jax import lax
from jax.experimental import pallas as pl
from jax.experimental.pallas import tpu as pltpu
from jax.sharding import PartitionSpec as P

MESH = pl.DeviceIdType.MESH
GROUPS = 2
NN = (((1,), (0,)), ((), ()))
NT = (((1,), (1,)), ((), ()))


def split(value):
    high = value.astype(jnp.bfloat16)
    return high, (value - high.astype(jnp.float32)).astype(jnp.bfloat16)


def dot3(left, right, dims):
    def one(a, b):
        return lax.dot_general(a, b, dims, preferred_element_type=jnp.float32)

    return one(left[0], right[0]) + (one(left[0], right[1]) + one(left[1], right[0]))


def flip(number, mask):
    bit = 1
    while bit <= mask:
        if mask & bit:
            number = number + (1 - 2 * (number // bit % 2)) * bit
        bit *= 2
    return number


def coef_kernel(
    n, leaf, rank,
    rs_hbm, inv_hbm, vm_hbm, ym_hbm, mid_cap, vt_hbm, top_cap,
    field_out, coef_out,
    rs, inv, vm, vt, ym, cap, tcap, field,
    inv_h, inv_l, v_h, v_l, cap_h, cap_l, tcap_h, tcap_l, d_h, d_l,
    part, part_in, chip_sum, chip_in, pair, top_p, coef,
    d_part, d_part_in, d_sum, d_in, d_full,
    load_sem, cap_sem, out_sem, send_sem, recv_sem,
):
    m = n // 4
    chips = m // 2
    me = lax.axis_index("rows")
    quarter, place = me // m, me % m
    core, chip = place % 2, place // 2
    half, side = quarter // 2, quarter % 2
    partner = me + 1 - 2 * core
    sibling = me + m * (1 - 2 * side)
    across = me + 2 * m * (1 - 2 * half)
    rows, rhs = rs.shape
    blocks = rows // leaf
    cols = rhs // GROUPS
    hr = cols // 2
    w = cols // m
    wd = rank // m
    hd = rank // 2

    def on_chip(d):
        return me + 2 * (flip(chip, d) - chip)

    def ds(start, size):
        return pl.ds(pl.multiple_of(start, 8), size)

    loads = ((ym_hbm, ym), (vt_hbm, vt), (inv_hbm, inv), (rs_hbm, rs), (vm_hbm, vm))

    def load(k, b):
        src, dst = loads[k]
        at = pl.ds(b * leaf, leaf)
        return pltpu.make_async_copy(src.at[at], dst.at[at], load_sem.at[k, b])

    for b in range(blocks):
        load(0, b).start()
        load(1, b).start()
    for b in range(blocks):
        for k in (2, 3, 4):
            load(k, b).start()
    cap_copy = pltpu.make_async_copy(mid_cap.at[half], cap, cap_sem.at[0])
    tcap_copy = pltpu.make_async_copy(
        top_cap.at[0, ds(half * rank, rank)], tcap, cap_sem.at[1]
    )
    cap_copy.start()
    tcap_copy.start()

    barrier = pltpu.get_barrier_semaphore()
    peers = [partner, sibling, across] + [on_chip(d) for d in range(1, chips)]
    for peer in peers:
        pl.semaphore_signal(barrier, inc=1, device_id=(peer,), device_id_type=MESH)

    used = iter(range(send_sem.shape[0]))

    def send(src, dst, device):
        at = next(used)
        copy = pltpu.make_async_remote_copy(
            src_ref=src, dst_ref=dst, send_sem=send_sem.at[at], recv_sem=recv_sem.at[at],
            device_id=(device,), device_id_type=MESH,
        )
        copy.start()
        return copy

    def spread(view):
        return [send(view, view, on_chip(d)) for d in reversed(range(1, chips))]

    def wait(copies):
        for copy in copies:
            copy.wait()

    d_part[...] = jnp.zeros_like(d_part)

    def d_step(b, _):
        at = ds(b * leaf, leaf)
        load(0, b).wait()
        load(1, b).wait()
        v = split(vt[at, :])
        v_h[at, rank:], v_l[at, rank:] = v
        d_part[...] += dot3(split(ym[at, :].T), v, NN)
        return 0

    lax.fori_loop(0, blocks, d_step, 0)
    pl.semaphore_wait(barrier, len(peers))
    d_a = send(d_part.at[ds((1 - core) * hd, hd)], d_part_in, partner)

    def leaf_step(g, b):
        at = ds(b * leaf, leaf)
        here = slice(g * cols, (g + 1) * cols)
        if g == 0:
            for k in (2, 3, 4):
                load(k, b).wait()
            inv_h[at, :], inv_l[at, :] = split(inv[at, :])
            v_h[at, :rank], v_l[at, :rank] = split(vm[at, :])
        out = dot3((inv_h[at, :], inv_l[at, :]), split(rs[at, here]), NN)
        field[at, here] = out
        part[g] += dot3(split(out.T), (v_h[at, :], v_l[at, :]), NN)

    def leaf_run(g, first, last):
        def step(b, _):
            leaf_step(g, b)
            return 0

        lax.fori_loop(first, last, step, 0)

    def give_partner(g):
        return send(part.at[g, ds((1 - core) * hr, hr)], part_in.at[g], partner)

    def give_chips(g):
        chip_sum[g] = part[g, ds(core * hr, hr), :] + part_in[g]
        return [
            send(chip_sum.at[g, ds(flip(chip, d) * w, w)], chip_in.at[g, d], on_chip(d))
            for d in reversed(range(1, chips))
        ]

    def give_sibling(g):
        total = chip_sum[g, ds(chip * w, w), :]
        for d in range(1, chips):
            total += chip_in[g, d]
        pair[g, side] = total
        return send(pair.at[g, side], pair.at[g, side], sibling)

    def own(g):
        return ds(g * cols + (core * chips + chip) * w, w)

    def core_rows(g):
        return ds(g * cols + core * hr, hr)

    part[...] = jnp.zeros_like(part)
    leaf_run(0, 0, blocks)
    a0 = give_partner(0)
    d_a.wait()
    d_sum[...] = d_part[ds(core * hd, hd), :] + d_part_in[...]
    d_b = [
        send(d_sum.at[ds(flip(chip, d) * wd, wd)], d_in.at[d], on_chip(d))
        for d in reversed(range(1, chips))
    ]
    leaf_run(1, 0, blocks // 2)
    a0.wait()
    b0 = give_chips(0)
    wait(d_b)
    d_total = d_sum[ds(chip * wd, wd), :]
    for d in range(1, chips):
        d_total += d_in[d]
    d_own = ds((core * chips + chip) * wd, wd)
    d_full[side, d_own, :] = d_total
    d_z = send(d_full.at[side, d_own], d_full.at[side, d_own], sibling)
    leaf_run(1, blocks // 2, blocks)
    a1 = give_partner(1)
    field_copy = pltpu.make_async_copy(field, field_out, out_sem.at[0])
    field_copy.start()
    wait(b0)
    c0 = give_sibling(0)
    d_z.wait()
    d_ag = spread(d_full.at[:, d_own])
    a1.wait()
    b1 = give_chips(1)
    cap_copy.wait()
    tcap_copy.wait()
    cap_h[...], cap_l[...] = split(cap[...])
    tcap_h[...], tcap_l[...] = split(tcap[...])

    def middle(g):
        stacked = jnp.concatenate([pair[g, 1, :, :rank], pair[g, 0, :, :rank]], axis=1)
        both = dot3(split(stacked), (cap_h[...], cap_l[...]), NT)
        coef[own(g), :rank] = jnp.where(side == 0, both[:, :rank], both[:, rank:])
        return both, spread(coef.at[own(g), pl.ds(0, rank)])

    def give_across(g, both):
        total = pair[g, 0, :, rank:] + pair[g, 1, :, rank:]
        total -= dot3(split(both), (d_h[...], d_l[...]), NN)
        top_p[g, half] = total
        return send(top_p.at[g, half], top_p.at[g, half], across)

    def top(g):
        stacked = jnp.concatenate([top_p[g, 1], top_p[g, 0]], axis=1)
        coef[own(g), rank:] = dot3(split(stacked), (tcap_h[...], tcap_l[...]), NT)
        return spread(coef.at[own(g), pl.ds(rank, rank)])

    def forward(g, first):
        view = coef.at[core_rows(g), pl.ds(first, rank)]
        return send(view, view, partner)

    c0.wait()
    both0, mid0 = middle(0)
    wait(d_ag)
    d_half = d_full.at[:, ds(core * hd, hd)]
    d_f = send(d_half, d_half, partner)
    wait(b1)
    c1 = give_sibling(1)
    d_f.wait()
    for s in range(2):
        d_h[s * rank : (s + 1) * rank, :], d_l[s * rank : (s + 1) * rank, :] = split(d_full[s])
    x0 = give_across(0, both0)
    c1.wait()
    both1, mid1 = middle(1)
    x1 = give_across(1, both1)
    x0.wait()
    top0 = top(0)
    wait(mid0)
    f0 = forward(0, 0)
    x1.wait()
    top1 = top(1)
    wait(mid1)
    f1 = forward(1, 0)
    wait(top0)
    f2 = forward(0, rank)
    wait(top1)
    f3 = forward(1, rank)
    wait([f0, f1, f2, f3])
    coef_copy = pltpu.make_async_copy(coef, coef_out, out_sem.at[1])
    coef_copy.start()
    coef_copy.wait()
    field_copy.wait()


def coefficients(n, rs, inv, vm, ym, mid_cap, vt, top_cap):
    rows, rhs = rs.shape
    leaf = inv.shape[1]
    rank = vm.shape[1]
    m = n // 4
    chips = m // 2
    cols = rhs // GROUPS
    w, wd = cols // m, rank // m
    blocks = rows // leaf
    f32, bf16 = jnp.float32, jnp.bfloat16
    copies = 2 * chips + 2 + GROUPS * (3 * chips + 2)

    def vmem(*shape, dtype=f32):
        return pltpu.VMEM(shape, dtype)

    return pl.pallas_call(
        functools.partial(coef_kernel, n, leaf, rank),
        out_shape=(
            jax.ShapeDtypeStruct((rows, rhs), f32),
            jax.ShapeDtypeStruct((rhs, 2 * rank), f32),
        ),
        in_specs=[pl.BlockSpec(memory_space=pl.ANY)] * 7,
        out_specs=[pl.BlockSpec(memory_space=pl.ANY)] * 2,
        scratch_shapes=[
            vmem(rows, rhs), vmem(rows, leaf), vmem(rows, rank), vmem(rows, rank),
            vmem(rows, rank), vmem(2 * rank, 2 * rank), vmem(rank, 2 * rank), vmem(rows, rhs),
            vmem(rows, leaf, dtype=bf16), vmem(rows, leaf, dtype=bf16),
            vmem(rows, 2 * rank, dtype=bf16), vmem(rows, 2 * rank, dtype=bf16),
            vmem(2 * rank, 2 * rank, dtype=bf16), vmem(2 * rank, 2 * rank, dtype=bf16),
            vmem(rank, 2 * rank, dtype=bf16), vmem(rank, 2 * rank, dtype=bf16),
            vmem(2 * rank, rank, dtype=bf16), vmem(2 * rank, rank, dtype=bf16),
            vmem(GROUPS, cols, 2 * rank), vmem(GROUPS, cols // 2, 2 * rank),
            vmem(GROUPS, cols // 2, 2 * rank), vmem(GROUPS, chips, w, 2 * rank),
            vmem(GROUPS, 2, w, 2 * rank), vmem(GROUPS, 2, w, rank), vmem(rhs, 2 * rank),
            vmem(rank, rank), vmem(rank // 2, rank), vmem(rank // 2, rank),
            vmem(chips, wd, rank), vmem(2, rank, rank),
            pltpu.SemaphoreType.DMA((5, blocks)),
            pltpu.SemaphoreType.DMA((2,)),
            pltpu.SemaphoreType.DMA((2,)),
            pltpu.SemaphoreType.DMA((copies,)),
            pltpu.SemaphoreType.DMA((copies,)),
        ],
        compiler_params=pltpu.CompilerParams(
            collective_id=0, has_side_effects=True, vmem_limit_bytes=48 * 2**20
        ),
        name="coefficients",
    )(rs, inv, vm, ym, mid_cap, vt, top_cap)


def correct_kernel(field, ym, yt, coef, out, coef_h, coef_l):
    rank = ym.shape[1]

    @pl.when(pl.program_id(0) == 0)
    def _():
        coef_h[...], coef_l[...] = split(coef[...])

    fixing = dot3(split(ym[...]), (coef_h[:, :rank], coef_l[:, :rank]), NT)
    fixing += dot3(split(yt[...]), (coef_h[:, rank:], coef_l[:, rank:]), NT)
    out[...] = field[...] - fixing


def correct(field, ym, yt, coef):
    rows, rhs = field.shape
    rank = ym.shape[1]
    tile = 512
    return pl.pallas_call(
        correct_kernel,
        out_shape=jax.ShapeDtypeStruct((rows, rhs), jnp.float32),
        grid=(rows // tile,),
        in_specs=[
            pl.BlockSpec((tile, rhs), lambda i: (i, 0)),
            pl.BlockSpec((tile, rank), lambda i: (i, 0)),
            pl.BlockSpec((tile, rank), lambda i: (i, 0)),
            pl.BlockSpec((rhs, 2 * rank), lambda i: (0, 0)),
        ],
        out_specs=pl.BlockSpec((tile, rhs), lambda i: (i, 0)),
        scratch_shapes=[pltpu.VMEM((rhs, 2 * rank), jnp.bfloat16)] * 2,
        compiler_params=pltpu.CompilerParams(vmem_limit_bytes=32 * 2**20),
        name="correct",
    )(field, ym, yt, coef)


def per_device(
    n, right_sides, leaf_inverse, mid_proj, mid_basis, mid_cap, top_proj, top_basis, top_cap
):
    field, coef = coefficients(
        n, right_sides, leaf_inverse, mid_proj, mid_basis, mid_cap, top_proj, top_cap
    )
    return correct(field, mid_basis, top_basis, coef)


def solution(mesh):
    placed = (
        P("rows", None),
        P("rows", None),
        P("rows", None),
        P("rows", None),
        P(),
        P("rows", None),
        P("rows", None),
        P(),
    )
    return jax.shard_map(
        functools.partial(per_device, mesh.shape["rows"]),
        mesh=mesh,
        in_specs=placed,
        out_specs=P("rows", None),
        check_vma=False,
    )
```

time: 154 us -> 55.1 us (0.36)
  waiting for transfers between devices: 87.7 us -> 0 us
  Pallas kernels: 0 us -> 49.8 us
  matrix products: 39.3 us -> 0 us
  starting transfers between devices: 12.9 us -> 0 us
  local copies, waits for them, and re-layouts: 13.2 us -> 5.15 us
    ppermute x9 -> x0, waiting for transfers between devices: 87.7 us -> none  [partner(): return lax.ppermute(value, axis, pairs)]
    pallas_call x0 -> x2, Pallas kernels: none -> 49.8 us  [the longest x1 44.6 us: coefficients(): pl.pallas_call(functools.partial(coef_kernel, n, leaf, rank), out_shape=(...]
    dot_general x9 -> x0, matrix products: 39.3 us -> none  [the longest x1 10.2 us: per_device(): return mid_field - jnp.dot(top_basis, coef_top, precision=PRECISE)]
    ppermute x9 -> x0, starting transfers between devices: 12.9 us -> none  [partner(): return lax.ppermute(value, axis, pairs)]
    reshape x1 -> x0, local copies, waits for them, and re-layouts: 5.37 us -> none  [leaf_apply(): jnp.einsum('bij,bjr->bir', blocks, pieces, precision=PRECISE)]
    sub x1 -> x0, local copies, waits for them, and re-layouts: 5.34 us -> none  [per_device(): return mid_field - jnp.dot(top_basis, coef_top, precision=PRECISE)]
    unnamed x14 -> x10, local copies, waits for them, and re-layouts: 0.03 us -> 5.15 us
    dynamic_slice x2 -> x0, local copies, waits for them, and re-layouts: 2.48 us -> none  [couple(): lax.dynamic_slice_in_dim(matrix, upper_half * rank_size, rank_size, 0)]
  transfers between devices with their start and end apart: 9 -> 0, of which waited for: 9 -> 0; matrix products, arithmetic and copies ran while one was open for 5% -> 0% of each run, Pallas kernels for 0% -> 0%
where the time goes in v1:
time: 55.1 us; the launch traced here: 54.9 us
  Pallas kernels  49.8 us (90%)
  local copies, waits for them, and re-layouts  5.15 us (9%)
    pallas_call x1, Pallas kernels, coefficients(): pl.pallas_call(functools.partial(coef_kernel, n, leaf, rank), out_shape=(...  44.6 us
    pallas_call x1, Pallas kernels, correct(): pl.pallas_call(correct_kernel, out_shape=jax.ShapeDtypeStruct((rows, rhs)...  5.2 us
    unnamed x10, local copies, waits for them, and re-layouts  5.15 us

profile of v1, /device:TPU:0, one launch (start us, length us, event | category | flops | bytes accessed | tf_op | source)
XLA Modules:
  0.0 54.9 jit_solution(1391188731202208370)
XLA Ops:
  0.0 0.0 copy-start
  0.0 0.0 copy-start.2
  0.0 1.7 %copy-done.2 = f32[2048,256]{1,0:T(8,128)S(1)} copy-done((f32[2048,256]{1,0:T(8,128)S(1)}, f32[2048,256]{1,0:T(8,128)}, u32[]{:S(2)}) %copy-start.2) | copy-done | bytes 2097176
  1.7 0.0 copy-start.4
  1.7 1.2 %copy-done.4 = f32[1,512,512]{2,1,0:T(8,128)S(1)} copy-done((f32[1,512,512]{2,1,0:T(8,128)S(1)}, f32[1,512,512]{2,1,0:T(8,128)}, u32[]{:S(2)}) %copy-start.4) | copy-done | bytes 1048600
  3.0 0.0 copy-start.3
  3.0 44.6 %coefficients.1 = (f32[2048,512]{1,0:T(8,128)}, f32[512,512]{1,0:T(8,128)S(1)}) custom-call(f32[2048,512]{1,0:T(8,128)} %rs_hbm.1, f32[2048,512]{1,0:T(8,128)} %inv_hbm.1, f32[2048,256]{1,0:T(8,128)S(1)} %copy-done.2, f32[2048,256]{1,0:T(8,128)} %ym.1, f32[2,512,512]{2,1,0:T(8,128)} %mid_cap.1, f32[2048,256]{1,0:T(8,128)} %vt_hbm.1, f32[1,512,512]{2,1,0:T(8,128)S(1)} %copy-done.4), custom_call_target="tpu_custom_call" | custom-call | tf_op jit(solution)/shard_map/coefficients/pallas_call | solution.py:273
  47.5 0.0 copy-done
  47.5 0.0 copy-done.3
  47.6 0.0 copy-start.1
  47.6 2.2 %copy-done.1 = f32[2048,512]{1,0:T(8,128)S(1)} copy-done((f32[2048,512]{1,0:T(8,128)S(1)}, f32[2048,512]{1,0:T(8,128)}, u32[]{:S(2)}) %copy-start.1) | copy-done | bytes 4194328
  49.7 5.2 %correct.1 = f32[2048,512]{1,0:T(8,128)} custom-call(f32[2048,512]{1,0:T(8,128)S(1)} %copy-done.1, f32[2048,256]{1,0:T(8,128)S(1)} %copy-done, f32[2048,256]{1,0:T(8,128)S(1)} %copy-done.3, f32[512,512]{1,0:T(8,128)S(1)} %get-tuple-element.8.coef), custom_call_target="tpu_custom_call" | custom-call | tf_op jit(solution)/shard_map/correct/pallas_call | solution.py:323
Async XLA Ops:
  0.0 47.5 %copy-start = (f32[2048,256]{1,0:T(8,128)S(1)}, f32[2048,256]{1,0:T(8,128)}, u32[]{:S(2)}) copy-start(f32[2048,256]{1,0:T(8,128)} %ym.1) | copy-start | bytes 6291460
  0.0 1.7 %copy-start.2 = (f32[2048,256]{1,0:T(8,128)S(1)}, f32[2048,256]{1,0:T(8,128)}, u32[]{:S(2)}) copy-start(f32[2048,256]{1,0:T(8,128)} %vm_hbm.1) | copy-start | bytes 6291460
  1.7 1.2 %copy-start.4 = (f32[1,512,512]{2,1,0:T(8,128)S(1)}, f32[1,512,512]{2,1,0:T(8,128)}, u32[]{:S(2)}) copy-start(f32[1,512,512]{2,1,0:T(8,128)} %top_cap.1) | copy-start | bytes 3145732
  3.0 44.6 %copy-start.3 = (f32[2048,256]{1,0:T(8,128)S(1)}, f32[2048,256]{1,0:T(8,128)}, u32[]{:S(2)}) copy-start(f32[2048,256]{1,0:T(8,128)} %yt.1) | copy-start | bytes 6291460
  47.6 2.2 %copy-start.1 = (f32[2048,512]{1,0:T(8,128)S(1)}, f32[2048,512]{1,0:T(8,128)}, u32[]{:S(2)}) copy-start(f32[2048,512]{1,0:T(8,128)} %get-tuple-element.7.field) | copy-start | bytes 12582916

commit v2 on v0

v2 whole, which is shorter than its diff:
```python
import functools

import jax
import jax.numpy as jnp
from jax import lax
from jax.experimental import pallas as pl
from jax.experimental.pallas import tpu as pltpu
from jax.sharding import PartitionSpec as P

MESH = pl.DeviceIdType.MESH
GROUPS = 2
NN = (((1,), (0,)), ((), ()))
NT = (((1,), (1,)), ((), ()))


def split(value):
    high = value.astype(jnp.bfloat16)
    return high, (value - high.astype(jnp.float32)).astype(jnp.bfloat16)


def dot3(left, right, dims):
    def one(a, b):
        return lax.dot_general(a, b, dims, preferred_element_type=jnp.float32)

    return one(left[0], right[0]) + (one(left[0], right[1]) + one(left[1], right[0]))


def flip(number, mask):
    bit = 1
    while bit <= mask:
        if mask & bit:
            number = number + (1 - 2 * (number // bit % 2)) * bit
        bit *= 2
    return number


def coef_kernel(
    n, leaf, rank,
    rs_hbm, inv_hbm, vm_hbm, ym_hbm, mid_cap, vt_hbm, yt_hbm, top_cap,
    field, coef_last,
    rs, inv, vm, vt, ym, yt, cap, tcap,
    inv_h, inv_l, v_h, v_l, cap_h, cap_l, tcap_h, tcap_l, d_h, d_l,
    part, part_in, chip_sum, chip_in, pair, top_p, coef,
    d_part, d_part_in, d_sum, d_in, d_full,
    load_sem, cap_sem, send_sem, recv_sem,
):
    m = n // 4
    chips = m // 2
    me = lax.axis_index("rows")
    quarter, place = me // m, me % m
    core, chip = place % 2, place // 2
    half, side = quarter // 2, quarter % 2
    partner = me + 1 - 2 * core
    sibling = me + m * (1 - 2 * side)
    across = me + 2 * m * (1 - 2 * half)
    rows, rhs = rs.shape
    blocks = rows // leaf
    cols = rhs // GROUPS
    hr = cols // 2
    w = cols // m
    wd = rank // m
    hd = rank // 2

    def on_chip(d):
        return me + 2 * (flip(chip, d) - chip)

    def ds(start, size):
        return pl.ds(pl.multiple_of(start, 8), size)

    loads = (
        (ym_hbm, ym), (vt_hbm, vt), (inv_hbm, inv), (rs_hbm, rs), (vm_hbm, vm), (yt_hbm, yt)
    )

    def load(k, b):
        src, dst = loads[k]
        at = ds(b * leaf, leaf)
        return pltpu.make_async_copy(src.at[at], dst.at[at], load_sem.at[k, b])

    def load_caps():
        return [
            pltpu.make_async_copy(mid_cap.at[half], cap, cap_sem.at[0]),
            pltpu.make_async_copy(top_cap.at[0, ds(half * rank, rank)], tcap, cap_sem.at[1]),
        ]

    def start(copies):
        for copy in copies:
            copy.start()

    def wait(copies):
        for copy in copies:
            copy.wait()

    start([load(k, b) for b in range(blocks) for k in (0, 1)])
    start([load(k, b) for b in range(blocks) for k in (2, 3, 4)])
    start(load_caps())
    start([load(5, b) for b in range(blocks)])

    barrier = pltpu.get_barrier_semaphore()
    peers = [partner, sibling, across] + [on_chip(d) for d in range(1, chips)]
    for peer in peers:
        pl.semaphore_signal(barrier, inc=1, device_id=(peer,), device_id_type=MESH)

    places = {}

    def remote(key, src, dst, device):
        at = places.setdefault(key, len(places))
        return pltpu.make_async_remote_copy(
            src_ref=src, dst_ref=dst, send_sem=send_sem.at[at], recv_sem=recv_sem.at[at],
            device_id=(device,), device_id_type=MESH,
        )

    others = tuple(reversed(range(1, chips)))

    def spread(key, view):
        return [remote((key, d), view, view, on_chip(d)) for d in others]

    def same(key, view, device):
        return [remote(key, view, view, device)]

    def d_own():
        return ds((core * chips + chip) * wd, wd)

    def d_core():
        return [remote("da", d_part.at[ds((1 - core) * hd, hd)], d_part_in, partner)]

    def d_chips():
        return [
            remote(("db", d), d_sum.at[ds(flip(chip, d) * wd, wd)], d_in.at[d], on_chip(d))
            for d in others
        ]

    def d_sibling():
        return same("dz", d_full.at[side, d_own()], sibling)

    def d_gather():
        return spread("dg", d_full.at[:, d_own()])

    def d_forward():
        return same("df", d_full.at[:, ds(core * hd, hd)], partner)

    def d_one():
        wait(d_core())
        d_sum[...] = d_part[ds(core * hd, hd), :] + d_part_in[...]
        start(d_chips())

    def d_two():
        wait(d_chips())
        total = d_sum[ds(chip * wd, wd), :]
        for d in others:
            total += d_in[d]
        d_full[side, d_own(), :] = total
        start(d_sibling())

    def d_three():
        wait(d_sibling())
        start(d_gather())

    def d_four():
        wait(d_gather())
        start(d_forward())

    def d_five():
        wait(d_forward())
        for s in range(2):
            at = slice(s * rank, (s + 1) * rank)
            d_h[at, :], d_l[at, :] = split(d_full[s])

    def to_core(g):
        return [remote(("a", g), part.at[g, ds((1 - core) * hr, hr)], part_in.at[g], partner)]

    def to_chips(g):
        return [
            remote(
                ("b", g, d), chip_sum.at[g, ds(flip(chip, d) * w, w)], chip_in.at[g, d], on_chip(d)
            )
            for d in others
        ]

    def to_sibling(g):
        return same(("c", g), pair.at[g, side], sibling)

    def to_across(g):
        return same(("x", g), top_p.at[g, half], across)

    def own(g):
        return ds(g * cols + (core * chips + chip) * w, w)

    def gather(g, level):
        return spread(("g", g, level), coef.at[own(g), pl.ds(level * rank, rank)])

    def forward(g, level):
        view = coef.at[ds(g * cols + core * hr, hr), pl.ds(level * rank, rank)]
        return same(("f", g, level), view, partner)

    def add_core(g):
        wait(to_core(g))
        chip_sum[g] = part[g, ds(core * hr, hr), :] + part_in[g]
        start(to_chips(g))

    def add_chips(g):
        wait(to_chips(g))
        total = chip_sum[g, ds(chip * w, w), :]
        for d in others:
            total += chip_in[g, d]
        pair[g, side] = total
        start(to_sibling(g))

    def middle(g):
        wait(to_sibling(g))
        stacked = jnp.concatenate([pair[g, 1, :, :rank], pair[g, 0, :, :rank]], axis=1)
        both = dot3(split(stacked), (cap_h[...], cap_l[...]), NT)
        coef[own(g), :rank] = jnp.where(side == 0, both[:, :rank], both[:, rank:])
        return both

    def cross(g, both):
        total = pair[g, 0, :, rank:] + pair[g, 1, :, rank:]
        top_p[g, half] = total - dot3(split(both), (d_h[...], d_l[...]), NN)
        start(to_across(g))

    def top(g):
        wait(to_across(g))
        stacked = jnp.concatenate([top_p[g, 1], top_p[g, 0]], axis=1)
        coef[own(g), rank:] = dot3(split(stacked), (tcap_h[...], tcap_l[...]), NT)
        start(gather(g, 1))

    def pass_on(g, level):
        wait(gather(g, level))
        start(forward(g, level))

    def correct_group(g, level):
        wait(forward(g, level))
        here = slice(g * cols, (g + 1) * cols)
        factor = split(coef[here, level * rank : (level + 1) * rank])
        basis = (ym, yt)[level]

        def step(b, _):
            at = ds(b * leaf, leaf)
            field[at, here] -= dot3(split(basis[at, :]), factor, NT)
            return 0

        lax.fori_loop(0, blocks, step, 0)

    def leaf_run(g, hooks):
        here = slice(g * cols, (g + 1) * cols)

        def step(b, _):
            for when, hook in hooks:
                pl.when(b == when)(hook)
            at = ds(b * leaf, leaf)
            if g == 0:
                wait([load(k, b) for k in (2, 3, 4)])
                inv_h[at, :], inv_l[at, :] = split(inv[at, :])
                v_h[at, :rank], v_l[at, :rank] = split(vm[at, :])
            out = dot3((inv_h[at, :], inv_l[at, :]), split(rs[at, here]), NN)
            field[at, here] = out
            part[g] += dot3(split(out.T), (v_h[at, :], v_l[at, :]), NN)
            return 0

        lax.fori_loop(0, blocks, step, 0)

    def split_caps():
        wait(load_caps())
        cap_h[...], cap_l[...] = split(cap[...])
        tcap_h[...], tcap_l[...] = split(tcap[...])

    d_part[...] = jnp.zeros_like(d_part)
    part[...] = jnp.zeros_like(part)

    def d_step(b, _):
        at = ds(b * leaf, leaf)
        wait([load(0, b), load(1, b)])
        v = split(vt[at, :])
        v_h[at, rank:], v_l[at, rank:] = v
        d_part[...] += dot3(split(ym[at, :].T), v, NN)
        return 0

    lax.fori_loop(0, blocks, d_step, 0)
    pl.semaphore_wait(barrier, len(peers))
    start(d_core())
    leaf_run(0, ((1, d_one), (blocks - 1, d_two)))
    start(to_core(0))
    d_three()
    leaf_run(1, ((1, lambda: add_core(0)), (2, d_four), (blocks - 1, lambda: add_chips(0))))
    start(to_core(1))
    split_caps()
    add_core(1)
    both = middle(0)
    start(gather(0, 0))
    d_five()
    cross(0, both)
    add_chips(1)
    top(0)
    both = middle(1)
    cross(1, both)
    start(gather(1, 0))
    pass_on(0, 0)
    wait([load(5, b) for b in range(blocks)])
    correct_group(0, 0)
    top(1)
    pass_on(0, 1)
    pass_on(1, 0)
    correct_group(0, 1)
    pass_on(1, 1)
    correct_group(1, 0)
    wait(forward(1, 1))
    coef_last[...] = coef[cols:, rank:]


def coefficients(n, rs, inv, vm, ym, mid_cap, vt, yt, top_cap):
    rows, rhs = rs.shape
    leaf = inv.shape[1]
    rank = vm.shape[1]
    m = n // 4
    chips = m // 2
    cols = rhs // GROUPS
    w, wd = cols // m, rank // m
    blocks = rows // leaf
    f32, bf16 = jnp.float32, jnp.bfloat16
    copies = 2 * chips + 2 + GROUPS * (3 * chips + 2)

    def vmem(*shape, dtype=f32):
        return pltpu.VMEM(shape, dtype)

    return pl.pallas_call(
        functools.partial(coef_kernel, n, leaf, rank),
        out_shape=(vmem(rows, rhs), vmem(cols, rank)),
        in_specs=[pl.BlockSpec(memory_space=pltpu.HBM)] * 8,
        out_specs=[pl.BlockSpec(memory_space=pltpu.VMEM)] * 2,
        scratch_shapes=[
            vmem(rows, rhs), vmem(rows, leaf), vmem(rows, rank), vmem(rows, rank),
            vmem(rows, rank), vmem(rows, rank), vmem(2 * rank, 2 * rank), vmem(rank, 2 * rank),
            vmem(rows, leaf, dtype=bf16), vmem(rows, leaf, dtype=bf16),
            vmem(rows, 2 * rank, dtype=bf16), vmem(rows, 2 * rank, dtype=bf16),
            vmem(2 * rank, 2 * rank, dtype=bf16), vmem(2 * rank, 2 * rank, dtype=bf16),
            vmem(rank, 2 * rank, dtype=bf16), vmem(rank, 2 * rank, dtype=bf16),
            vmem(2 * rank, rank, dtype=bf16), vmem(2 * rank, rank, dtype=bf16),
            vmem(GROUPS, cols, 2 * rank), vmem(GROUPS, cols // 2, 2 * rank),
            vmem(GROUPS, cols // 2, 2 * rank), vmem(GROUPS, chips, w, 2 * rank),
            vmem(GROUPS, 2, w, 2 * rank), vmem(GROUPS, 2, w, rank), vmem(rhs, 2 * rank),
            vmem(rank, rank), vmem(rank // 2, rank), vmem(rank // 2, rank),
            vmem(chips, wd, rank), vmem(2, rank, rank),
            pltpu.SemaphoreType.DMA((6, blocks)),
            pltpu.SemaphoreType.DMA((2,)),
            pltpu.SemaphoreType.DMA((copies,)),
            pltpu.SemaphoreType.DMA((copies,)),
        ],
        compiler_params=pltpu.CompilerParams(
            collective_id=0, has_side_effects=True, vmem_limit_bytes=44 * 2**20
        ),
        name="coefficients",
    )(rs, inv, vm, ym, mid_cap, vt, yt, top_cap)


def finish_kernel(field, yt, coef, out, last, sem):
    rows, rhs = out.shape
    cols = coef.shape[0]
    done = rhs - cols
    tile = rows // 4
    left = pltpu.make_async_copy(
        field.at[:, pl.ds(0, done)], out.at[:, pl.ds(0, done)], sem.at[4]
    )
    left.start()
    factor = split(coef[...])
    copies = []
    for i in range(4):
        at = slice(i * tile, (i + 1) * tile)
        last[at, :] = field[at, done:] - dot3(split(yt[at, :]), factor, NT)
        copy = pltpu.make_async_copy(
            last.at[pl.ds(i * tile, tile)],
            out.at[pl.ds(i * tile, tile), pl.ds(done, cols)],
            sem.at[i],
        )
        copy.start()
        copies.append(copy)
    left.wait()
    for copy in copies:
        copy.wait()


def finish(field, yt, coef):
    rows, rhs = field.shape
    return pl.pallas_call(
        finish_kernel,
        out_shape=jax.ShapeDtypeStruct((rows, rhs), jnp.float32),
        in_specs=[pl.BlockSpec(memory_space=pltpu.VMEM)] * 3,
        out_specs=pl.BlockSpec(memory_space=pltpu.HBM),
        scratch_shapes=[
            pltpu.VMEM((rows, coef.shape[0]), jnp.float32),
            pltpu.SemaphoreType.DMA((5,)),
        ],
        compiler_params=pltpu.CompilerParams(vmem_limit_bytes=16 * 2**20),
        name="finish",
    )(field, yt, coef)


def per_device(
    n, right_sides, leaf_inverse, mid_proj, mid_basis, mid_cap, top_proj, top_basis, top_cap
):
    field, coef = coefficients(
        n, right_sides, leaf_inverse, mid_proj, mid_basis, mid_cap, top_proj, top_basis, top_cap
    )
    return finish(field, top_basis, coef)


def solution(mesh):
    placed = (
        P("rows", None),
        P("rows", None),
        P("rows", None),
        P("rows", None),
        P(),
        P("rows", None),
        P("rows", None),
        P(),
    )
    return jax.shard_map(
        functools.partial(per_device, mesh.shape["rows"]),
        mesh=mesh,
        in_specs=placed,
        out_specs=P("rows", None),
        check_vma=False,
    )
```

time: 154 us -> 51.8 us (0.34)
  waiting for transfers between devices: 87.7 us -> 0 us
  Pallas kernels: 0 us -> 47 us
  matrix products: 39.3 us -> 0 us
  starting transfers between devices: 12.9 us -> 0 us
  local copies, waits for them, and re-layouts: 13.2 us -> 4.56 us
    ppermute x9 -> x0, waiting for transfers between devices: 87.7 us -> none  [partner(): return lax.ppermute(value, axis, pairs)]
    pallas_call x0 -> x2, Pallas kernels: none -> 47 us  [the longest x1 44.9 us: coefficients(): pl.pallas_call(functools.partial(coef_kernel, n, leaf, rank), out_shape=(...]
    dot_general x9 -> x0, matrix products: 39.3 us -> none  [the longest x1 10.2 us: per_device(): return mid_field - jnp.dot(top_basis, coef_top, precision=PRECISE)]
    ppermute x9 -> x0, starting transfers between devices: 12.9 us -> none  [partner(): return lax.ppermute(value, axis, pairs)]
    reshape x1 -> x0, local copies, waits for them, and re-layouts: 5.37 us -> none  [leaf_apply(): jnp.einsum('bij,bjr->bir', blocks, pieces, precision=PRECISE)]
    sub x1 -> x0, local copies, waits for them, and re-layouts: 5.34 us -> none  [per_device(): return mid_field - jnp.dot(top_basis, coef_top, precision=PRECISE)]
    unnamed x14 -> x8, local copies, waits for them, and re-layouts: 0.03 us -> 4.56 us
    dynamic_slice x2 -> x0, local copies, waits for them, and re-layouts: 2.48 us -> none  [couple(): lax.dynamic_slice_in_dim(matrix, upper_half * rank_size, rank_size, 0)]
  transfers between devices with their start and end apart: 9 -> 0, of which waited for: 9 -> 0; matrix products, arithmetic and copies ran while one was open for 5% -> 0% of each run, Pallas kernels for 0% -> 0%
where the time goes in v2:
time: 51.8 us; the launch traced here: 51.6 us
  Pallas kernels  47 us (91%)
  local copies, waits for them, and re-layouts  4.56 us (9%)
    pallas_call x1, Pallas kernels, coefficients(): pl.pallas_call(functools.partial(coef_kernel, n, leaf, rank), out_shape=(...  44.9 us
    unnamed x8, local copies, waits for them, and re-layouts  4.56 us
    pallas_call x1, Pallas kernels, finish(): pl.pallas_call(finish_kernel, out_shape=jax.ShapeDtypeStruct((rows, rhs),...  2.13 us

profile of v2, /device:TPU:0, one launch (start us, length us, event | category | flops | bytes accessed | tf_op | source)
XLA Modules:
  0.0 51.6 jit_solution(15635964163324966029)
XLA Ops:
  0.0 0.0 copy-start
  0.0 0.0 copy-start.1
  0.0 1.7 %copy-done.1 = f32[2048,256]{1,0:T(8,128)S(1)} copy-done((f32[2048,256]{1,0:T(8,128)S(1)}, f32[2048,256]{1,0:T(8,128)}, u32[]{:S(2)}) %copy-start.1) | copy-done | bytes 2097176
  1.7 0.0 copy-start.2
  1.7 1.6 %copy-done.2 = f32[2048,256]{1,0:T(8,128)S(1)} copy-done((f32[2048,256]{1,0:T(8,128)S(1)}, f32[2048,256]{1,0:T(8,128)}, u32[]{:S(2)}) %copy-start.2) | copy-done | bytes 2097176
  3.3 0.0 copy-start.3
  3.3 1.2 %copy-done.3 = f32[1,512,512]{2,1,0:T(8,128)S(1)} copy-done((f32[1,512,512]{2,1,0:T(8,128)S(1)}, f32[1,512,512]{2,1,0:T(8,128)}, u32[]{:S(2)}) %copy-start.3) | copy-done | bytes 1048600
  4.6 44.9 %coefficients.1 = (f32[2048,512]{1,0:T(8,128)S(1)}, f32[256,256]{1,0:T(8,128)S(1)}) custom-call(f32[2048,512]{1,0:T(8,128)} %rs_hbm.1, f32[2048,512]{1,0:T(8,128)} %inv_hbm.1, f32[2048,256]{1,0:T(8,128)S(1)} %copy-done.1, f32[2048,256]{1,0:T(8,128)S(1)} %copy-done.2, f32[2,512,512]{2,1,0:T(8,128)} %mid_cap.1, f32[2048,256]{1,0:T(8,128)} %vt_hbm.1, ...), custom_call_target="tpu_custom_call" | custom-call | tf_op jit(solution)/shard_map/coefficients/pallas_call | solution.py:324
  49.4 0.0 copy-done
  49.5 2.1 %finish.1 = f32[2048,512]{1,0:T(8,128)} custom-call(f32[2048,512]{1,0:T(8,128)S(1)} %get-tuple-element.7.field, f32[2048,256]{1,0:T(8,128)S(1)} %copy-done, f32[256,256]{1,0:T(8,128)S(1)} %get-tuple-element.8.coef), custom_call_target="tpu_custom_call" | custom-call | tf_op jit(solution)/shard_map/finish/pallas_call | solution.py:382
Async XLA Ops:
  0.0 49.4 %copy-start = (f32[2048,256]{1,0:T(8,128)S(1)}, f32[2048,256]{1,0:T(8,128)}, u32[]{:S(2)}) copy-start(f32[2048,256]{1,0:T(8,128)} %yt.1) | copy-start | bytes 6291460
  0.0 1.7 %copy-start.1 = (f32[2048,256]{1,0:T(8,128)S(1)}, f32[2048,256]{1,0:T(8,128)}, u32[]{:S(2)}) copy-start(f32[2048,256]{1,0:T(8,128)} %vm_hbm.1) | copy-start | bytes 6291460
  1.7 1.6 %copy-start.2 = (f32[2048,256]{1,0:T(8,128)S(1)}, f32[2048,256]{1,0:T(8,128)}, u32[]{:S(2)}) copy-start(f32[2048,256]{1,0:T(8,128)} %ym_hbm.1) | copy-start | bytes 6291460
  3.3 1.2 %copy-start.3 = (f32[1,512,512]{2,1,0:T(8,128)S(1)}, f32[1,512,512]{2,1,0:T(8,128)}, u32[]{:S(2)}) copy-start(f32[1,512,512]{2,1,0:T(8,128)} %top_cap.1) | copy-start | bytes 3145732

commit v3 on v2

--- a/solution.py
+++ b/solution.py
@@ -18,11 +18,18 @@
     return high, (value - high.astype(jnp.float32)).astype(jnp.bfloat16)
 
 
-def dot3(left, right, dims):
-    def one(a, b):
-        return lax.dot_general(a, b, dims, preferred_element_type=jnp.float32)
-
-    return one(left[0], right[0]) + (one(left[0], right[1]) + one(left[1], right[0]))
+def left3(value, axis=1):
+    high, low = split(value)
+    return jnp.concatenate([high, high, low], axis=axis)
+
+
+def right3(value, axis):
+    high, low = split(value)
+    return jnp.concatenate([high, low, high], axis=axis)
+
+
+def dot(left, right, dims):
+    return lax.dot_general(left, right, dims, preferred_element_type=jnp.float32)
 
 
 def flip(number, mask):
@@ -39,8 +46,8 @@
     rs_hbm, inv_hbm, vm_hbm, ym_hbm, mid_cap, vt_hbm, yt_hbm, top_cap,
     field, coef_last,
     rs, inv, vm, vt, ym, yt, cap, tcap,
-    inv_h, inv_l, v_h, v_l, cap_h, cap_l, tcap_h, tcap_l, d_h, d_l,
-    part, part_in, chip_sum, chip_in, pair, top_p, coef,
+    inv3, v3, cap3, tcap3, d3,
+    proj, part, part_in, chip_sum, chip_in, pair, top_p, coef,
     d_part, d_part_in, d_sum, d_in, d_full,
     load_sem, cap_sem, send_sem, recv_sem,
 ):
@@ -161,9 +168,7 @@
 
     def d_five():
         wait(d_forward())
-        for s in range(2):
-            at = slice(s * rank, (s + 1) * rank)
-            d_h[at, :], d_l[at, :] = split(d_full[s])
+        d3[...] = right3(jnp.concatenate([d_full[0], d_full[1]], axis=1), 1)
 
     def to_core(g):
         return [remote(("a", g), part.at[g, ds((1 - core) * hr, hr)], part_in.at[g], partner)]
@@ -208,19 +213,19 @@
     def middle(g):
         wait(to_sibling(g))
         stacked = jnp.concatenate([pair[g, 1, :, :rank], pair[g, 0, :, :rank]], axis=1)
-        both = dot3(split(stacked), (cap_h[...], cap_l[...]), NT)
+        both = dot(left3(stacked), cap3[...], NT)
         coef[own(g), :rank] = jnp.where(side == 0, both[:, :rank], both[:, rank:])
         return both
 
     def cross(g, both):
         total = pair[g, 0, :, rank:] + pair[g, 1, :, rank:]
-        top_p[g, half] = total - dot3(split(both), (d_h[...], d_l[...]), NN)
+        top_p[g, half] = total - dot(left3(both), d3[...], NT)
         start(to_across(g))
 
     def top(g):
         wait(to_across(g))
         stacked = jnp.concatenate([top_p[g, 1], top_p[g, 0]], axis=1)
-        coef[own(g), rank:] = dot3(split(stacked), (tcap_h[...], tcap_l[...]), NT)
+        coef[own(g), rank:] = dot(left3(stacked), tcap3[...], NT)
         start(gather(g, 1))
 
     def pass_on(g, level):
@@ -230,12 +235,12 @@
     def correct_group(g, level):
         wait(forward(g, level))
         here = slice(g * cols, (g + 1) * cols)
-        factor = split(coef[here, level * rank : (level + 1) * rank])
+        factor = right3(coef[here, level * rank : (level + 1) * rank], 1)
         basis = (ym, yt)[level]
 
         def step(b, _):
             at = ds(b * leaf, leaf)
-            field[at, here] -= dot3(split(basis[at, :]), factor, NT)
+            field[at, here] -= dot(left3(basis[at, :]), factor, NT)
             return 0
 
         lax.fori_loop(0, blocks, step, 0)
@@ -243,46 +248,57 @@
     def leaf_run(g, hooks):
         here = slice(g * cols, (g + 1) * cols)
 
-        def step(b, _):
+        def step(i, _):
             for when, hook in hooks:
-                pl.when(b == when)(hook)
-            at = ds(b * leaf, leaf)
-            if g == 0:
-                wait([load(k, b) for k in (2, 3, 4)])
-                inv_h[at, :], inv_l[at, :] = split(inv[at, :])
-                v_h[at, :rank], v_l[at, :rank] = split(vm[at, :])
-            out = dot3((inv_h[at, :], inv_l[at, :]), split(rs[at, here]), NN)
-            field[at, here] = out
-            part[g] += dot3(split(out.T), (v_h[at, :], v_l[at, :]), NN)
+                pl.when(i == when)(hook)
+            outs = []
+            for b in (2 * i, 2 * i + 1):
+                at = ds(b * leaf, leaf)
+                if g == 0:
+                    wait([load(k, b) for k in (2, 3, 4)])
+                    inv3[at, :] = left3(inv[at, :])
+                    v3[b, :rank, :] = left3(vm[at, :].T)
+                out = dot(inv3[at, :], right3(rs[at, here], 0), NN)
+                field[at, here] = out
+                outs.append(right3(out, 0))
+            proj[...] += dot(v3[2 * i], outs[0], NN) + dot(v3[2 * i + 1], outs[1], NN)
             return 0
 
-        lax.fori_loop(0, blocks, step, 0)
+        proj[...] = jnp.zeros_like(proj)
+        lax.fori_loop(0, blocks // 2, step, 0)
+        part[g] = proj[...].T
 
     def split_caps():
         wait(load_caps())
-        cap_h[...], cap_l[...] = split(cap[...])
-        tcap_h[...], tcap_l[...] = split(tcap[...])
+        cap3[...] = right3(cap[...], 1)
+        tcap3[...] = right3(tcap[...], 1)
 
     d_part[...] = jnp.zeros_like(d_part)
-    part[...] = jnp.zeros_like(part)
 
     def d_step(b, _):
         at = ds(b * leaf, leaf)
         wait([load(0, b), load(1, b)])
-        v = split(vt[at, :])
-        v_h[at, rank:], v_l[at, rank:] = v
-        d_part[...] += dot3(split(ym[at, :].T), v, NN)
+        v = left3(vt[at, :].T)
+        v3[b, rank:, :] = v
+        d_part[...] += dot(v, right3(ym[at, :], 0), NN)
         return 0
 
     lax.fori_loop(0, blocks, d_step, 0)
     pl.semaphore_wait(barrier, len(peers))
     start(d_core())
-    leaf_run(0, ((1, d_one), (blocks - 1, d_two)))
+    leaf_run(0, ((1, d_one),))
     start(to_core(0))
-    d_three()
-    leaf_run(1, ((1, lambda: add_core(0)), (2, d_four), (blocks - 1, lambda: add_chips(0))))
+    d_two()
+    split_caps()
+
+    def between():
+        add_core(0)
+        d_three()
+
+    leaf_run(1, ((1, between),))
     start(to_core(1))
-    split_caps()
+    add_chips(0)
+    d_four()
     add_core(1)
     both = middle(0)
     start(gather(0, 0))
@@ -329,11 +345,9 @@
         scratch_shapes=[
             vmem(rows, rhs), vmem(rows, leaf), vmem(rows, rank), vmem(rows, rank),
             vmem(rows, rank), vmem(rows, rank), vmem(2 * rank, 2 * rank), vmem(rank, 2 * rank),
-            vmem(rows, leaf, dtype=bf16), vmem(rows, leaf, dtype=bf16),
-            vmem(rows, 2 * rank, dtype=bf16), vmem(rows, 2 * rank, dtype=bf16),
-            vmem(2 * rank, 2 * rank, dtype=bf16), vmem(2 * rank, 2 * rank, dtype=bf16),
-            vmem(rank, 2 * rank, dtype=bf16), vmem(rank, 2 * rank, dtype=bf16),
-            vmem(2 * rank, rank, dtype=bf16), vmem(2 * rank, rank, dtype=bf16),
+            vmem(rows, 3 * leaf, dtype=bf16), vmem(blocks, 2 * rank, 3 * leaf, dtype=bf16),
+            vmem(2 * rank, 6 * rank, dtype=bf16), vmem(rank, 6 * rank, dtype=bf16),
+            vmem(rank, 6 * rank, dtype=bf16), vmem(2 * rank, cols),
             vmem(GROUPS, cols, 2 * rank), vmem(GROUPS, cols // 2, 2 * rank),
             vmem(GROUPS, cols // 2, 2 * rank), vmem(GROUPS, chips, w, 2 * rank),
             vmem(GROUPS, 2, w, 2 * rank), vmem(GROUPS, 2, w, rank), vmem(rhs, 2 * rank),
@@ -345,7 +359,7 @@
             pltpu.SemaphoreType.DMA((copies,)),
         ],
         compiler_params=pltpu.CompilerParams(
-            collective_id=0, has_side_effects=True, vmem_limit_bytes=44 * 2**20
+            collective_id=0, has_side_effects=True, vmem_limit_bytes=56 * 2**20
         ),
         name="coefficients",
     )(rs, inv, vm, ym, mid_cap, vt, yt, top_cap)
@@ -360,11 +374,11 @@
         field.at[:, pl.ds(0, done)], out.at[:, pl.ds(0, done)], sem.at[4]
     )
     left.start()
-    factor = split(coef[...])
+    factor = right3(coef[...], 1)
     copies = []
     for i in range(4):
         at = slice(i * tile, (i + 1) * tile)
-        last[at, :] = field[at, done:] - dot3(split(yt[at, :]), factor, NT)
+        last[at, :] = field[at, done:] - dot(left3(yt[at, :]), factor, NT)
         copy = pltpu.make_async_copy(
             last.at[pl.ds(i * tile, tile)],
             out.at[pl.ds(i * tile, tile), pl.ds(done, cols)],

time: 51.8 us -> 47.4 us (0.915)
  local copies, waits for them, and re-layouts: 4.56 us -> 0.01 us
    unnamed x8 -> x2, local copies, waits for them, and re-layouts: 4.56 us -> 0.01 us
where the time goes in v3:
time: 47.4 us; the launch traced here: 47.2 us
  Pallas kernels  47.2 us (100%)
    pallas_call x1, Pallas kernels, coefficients(): pl.pallas_call(functools.partial(coef_kernel, n, leaf, rank), out_shape=(...  45.1 us
    pallas_call x1, Pallas kernels, finish(): pl.pallas_call(finish_kernel, out_shape=jax.ShapeDtypeStruct((rows, rhs),...  2.12 us

profile of v3, /device:TPU:0, one launch (start us, length us, event | category | flops | bytes accessed | tf_op | source)
XLA Modules:
  0.0 47.2 jit_solution(6844310426961633488)
XLA Ops:
  0.0 0.0 copy-start
  0.0 45.1 %coefficients.1 = (f32[2048,512]{1,0:T(8,128)S(1)}, f32[256,256]{1,0:T(8,128)S(1)}) custom-call(f32[2048,512]{1,0:T(8,128)} %rs_hbm.1, f32[2048,512]{1,0:T(8,128)} %inv_hbm.1, f32[2048,256]{1,0:T(8,128)} %vm_hbm.1, f32[2048,256]{1,0:T(8,128)} %ym_hbm.1, f32[2,512,512]{2,1,0:T(8,128)} %mid_cap.1, f32[2048,256]{1,0:T(8,128)} %vt_hbm.1, f32[2048,256]{1,0:T(8,128)} %yt.1, ...), custom_call_target="tpu_custom_call" | custom-call | tf_op jit(solution)/shard_map/coefficients/pallas_call | solution.py:340
  45.1 0.0 copy-done
  45.1 2.1 %finish.1 = f32[2048,512]{1,0:T(8,128)} custom-call(f32[2048,512]{1,0:T(8,128)S(1)} %get-tuple-element.7.field, f32[2048,256]{1,0:T(8,128)S(1)} %copy-done, f32[256,256]{1,0:T(8,128)S(1)} %get-tuple-element.8.coef), custom_call_target="tpu_custom_call" | custom-call | tf_op jit(solution)/shard_map/finish/pallas_call | solution.py:396
Async XLA Ops:
  0.0 45.1 %copy-start = (f32[2048,256]{1,0:T(8,128)S(1)}, f32[2048,256]{1,0:T(8,128)}, u32[]{:S(2)}) copy-start(f32[2048,256]{1,0:T(8,128)} %yt.1) | copy-start | bytes 6291460

commit v4 on v3

--- a/solution.py
+++ b/solution.py
@@ -16,6 +16,19 @@
 def split(value):
     high = value.astype(jnp.bfloat16)
     return high, (value - high.astype(jnp.float32)).astype(jnp.bfloat16)
+
+
+def both_parts(value):
+    high, low = split(value)
+    return jnp.stack([high, low])
+
+
+def small_dot(value, parts, dims):
+    count = value.shape[0]
+    high = value.astype(jnp.bfloat16).astype(jnp.float32)
+    stacked = jnp.concatenate([high, value - high], axis=0).astype(jnp.bfloat16)
+    wide = dot(stacked, parts[0], dims)
+    return wide[:count] + (wide[count:] + dot(high.astype(jnp.bfloat16), parts[1], dims))
 
 
 def left3(value, axis=1):
@@ -44,9 +57,9 @@
 def coef_kernel(
     n, leaf, rank,
     rs_hbm, inv_hbm, vm_hbm, ym_hbm, mid_cap, vt_hbm, yt_hbm, top_cap,
-    field, coef_last,
-    rs, inv, vm, vt, ym, yt, cap, tcap,
-    inv3, v3, cap3, tcap3, d3,
+    field, yt, coef_last,
+    rs, inv, vm, vt, ym, cap, tcap,
+    inv3, v3, cap2, tcap2, d2,
     proj, part, part_in, chip_sum, chip_in, pair, top_p, coef,
     d_part, d_part_in, d_sum, d_in, d_full,
     load_sem, cap_sem, send_sem, recv_sem,
@@ -75,13 +88,17 @@
         return pl.ds(pl.multiple_of(start, 8), size)
 
     loads = (
-        (ym_hbm, ym), (vt_hbm, vt), (inv_hbm, inv), (rs_hbm, rs), (vm_hbm, vm), (yt_hbm, yt)
+        (ym_hbm, ym), (vt_hbm, vt), (inv_hbm, inv), (vm_hbm, vm), (yt_hbm, yt), (rs_hbm, rs)
     )
 
     def load(k, b):
         src, dst = loads[k]
         at = ds(b * leaf, leaf)
         return pltpu.make_async_copy(src.at[at], dst.at[at], load_sem.at[k, b])
+
+    def load_rs(g, b):
+        at = (ds(b * leaf, leaf), pl.ds(g * cols, cols))
+        return pltpu.make_async_copy(rs_hbm.at[at], rs.at[at], load_sem.at[5 + g, b])
 
     def load_caps():
         return [
@@ -98,9 +115,11 @@
             copy.wait()
 
     start([load(k, b) for b in range(blocks) for k in (0, 1)])
-    start([load(k, b) for b in range(blocks) for k in (2, 3, 4)])
+    for b in range(blocks):
+        start([load(2, b), load_rs(0, b), load(3, b)])
+    start([load_rs(1, b) for b in range(blocks)])
     start(load_caps())
-    start([load(5, b) for b in range(blocks)])
+    start([load(4, b) for b in range(blocks)])
 
     barrier = pltpu.get_barrier_semaphore()
     peers = [partner, sibling, across] + [on_chip(d) for d in range(1, chips)]
@@ -168,7 +187,7 @@
 
     def d_five():
         wait(d_forward())
-        d3[...] = right3(jnp.concatenate([d_full[0], d_full[1]], axis=1), 1)
+        d2[...] = both_parts(jnp.concatenate([d_full[0], d_full[1]], axis=1))
 
     def to_core(g):
         return [remote(("a", g), part.at[g, ds((1 - core) * hr, hr)], part_in.at[g], partner)]
@@ -213,19 +232,19 @@
     def middle(g):
         wait(to_sibling(g))
         stacked = jnp.concatenate([pair[g, 1, :, :rank], pair[g, 0, :, :rank]], axis=1)
-        both = dot(left3(stacked), cap3[...], NT)
+        both = small_dot(stacked, cap2, NT)
         coef[own(g), :rank] = jnp.where(side == 0, both[:, :rank], both[:, rank:])
         return both
 
     def cross(g, both):
         total = pair[g, 0, :, rank:] + pair[g, 1, :, rank:]
-        top_p[g, half] = total - dot(left3(both), d3[...], NT)
+        top_p[g, half] = total - small_dot(both, d2, NT)
         start(to_across(g))
 
     def top(g):
         wait(to_across(g))
         stacked = jnp.concatenate([top_p[g, 1], top_p[g, 0]], axis=1)
-        coef[own(g), rank:] = dot(left3(stacked), tcap3[...], NT)
+        coef[own(g), rank:] = small_dot(stacked, tcap2, NT)
         start(gather(g, 1))
 
     def pass_on(g, level):
@@ -255,9 +274,10 @@
             for b in (2 * i, 2 * i + 1):
                 at = ds(b * leaf, leaf)
                 if g == 0:
-                    wait([load(k, b) for k in (2, 3, 4)])
+                    wait([load(2, b), load(3, b)])
                     inv3[at, :] = left3(inv[at, :])
                     v3[b, :rank, :] = left3(vm[at, :].T)
+                wait([load_rs(g, b)])
                 out = dot(inv3[at, :], right3(rs[at, here], 0), NN)
                 field[at, here] = out
                 outs.append(right3(out, 0))
@@ -270,8 +290,8 @@
 
     def split_caps():
         wait(load_caps())
-        cap3[...] = right3(cap[...], 1)
-        tcap3[...] = right3(tcap[...], 1)
+        cap2[...] = both_parts(cap[...])
+        tcap2[...] = both_parts(tcap[...])
 
     d_part[...] = jnp.zeros_like(d_part)
 
@@ -306,11 +326,11 @@
     cross(0, both)
     add_chips(1)
     top(0)
+    pass_on(0, 0)
     both = middle(1)
     cross(1, both)
     start(gather(1, 0))
-    pass_on(0, 0)
-    wait([load(5, b) for b in range(blocks)])
+    wait([load(4, b) for b in range(blocks)])
     correct_group(0, 0)
     top(1)
     pass_on(0, 1)
@@ -339,21 +359,21 @@
 
     return pl.pallas_call(
         functools.partial(coef_kernel, n, leaf, rank),
-        out_shape=(vmem(rows, rhs), vmem(cols, rank)),
+        out_shape=(vmem(rows, rhs), vmem(rows, rank), vmem(cols, rank)),
         in_specs=[pl.BlockSpec(memory_space=pltpu.HBM)] * 8,
-        out_specs=[pl.BlockSpec(memory_space=pltpu.VMEM)] * 2,
+        out_specs=[pl.BlockSpec(memory_space=pltpu.VMEM)] * 3,
         scratch_shapes=[
             vmem(rows, rhs), vmem(rows, leaf), vmem(rows, rank), vmem(rows, rank),
-            vmem(rows, rank), vmem(rows, rank), vmem(2 * rank, 2 * rank), vmem(rank, 2 * rank),
+            vmem(rows, rank), vmem(2 * rank, 2 * rank), vmem(rank, 2 * rank),
             vmem(rows, 3 * leaf, dtype=bf16), vmem(blocks, 2 * rank, 3 * leaf, dtype=bf16),
-            vmem(2 * rank, 6 * rank, dtype=bf16), vmem(rank, 6 * rank, dtype=bf16),
-            vmem(rank, 6 * rank, dtype=bf16), vmem(2 * rank, cols),
+            vmem(2, 2 * rank, 2 * rank, dtype=bf16), vmem(2, rank, 2 * rank, dtype=bf16),
+            vmem(2, rank, 2 * rank, dtype=bf16), vmem(2 * rank, cols),
             vmem(GROUPS, cols, 2 * rank), vmem(GROUPS, cols // 2, 2 * rank),
             vmem(GROUPS, cols // 2, 2 * rank), vmem(GROUPS, chips, w, 2 * rank),
             vmem(GROUPS, 2, w, 2 * rank), vmem(GROUPS, 2, w, rank), vmem(rhs, 2 * rank),
             vmem(rank, rank), vmem(rank // 2, rank), vmem(rank // 2, rank),
             vmem(chips, wd, rank), vmem(2, rank, rank),
-            pltpu.SemaphoreType.DMA((6, blocks)),
+            pltpu.SemaphoreType.DMA((5 + GROUPS, blocks)),
             pltpu.SemaphoreType.DMA((2,)),
             pltpu.SemaphoreType.DMA((copies,)),
             pltpu.SemaphoreType.DMA((copies,)),
@@ -410,10 +430,10 @@
 def per_device(
     n, right_sides, leaf_inverse, mid_proj, mid_basis, mid_cap, top_proj, top_basis, top_cap
 ):
-    field, coef = coefficients(
+    field, basis, coef = coefficients(
         n, right_sides, leaf_inverse, mid_proj, mid_basis, mid_cap, top_proj, top_basis, top_cap
     )
-    return finish(field, top_basis, coef)
+    return finish(field, basis, coef)
 
 
 def solution(mesh):

time: 47.4 us -> 48.6 us (1.025)
  Pallas kernels: 47.2 us -> 48.4 us
    pallas_call x1, Pallas kernels: 45.1 us -> 46.3 us  [coefficients(): pl.pallas_call(functools.partial(coef_kernel, n, leaf, rank), out_shape=(...]
where the time goes in v4:
time: 48.6 us; the launch traced here: 48.4 us
  Pallas kernels  48.4 us (100%)
    pallas_call x1, Pallas kernels, coefficients(): pl.pallas_call(functools.partial(coef_kernel, n, leaf, rank), out_shape=(...  46.3 us
    pallas_call x1, Pallas kernels, finish(): pl.pallas_call(finish_kernel, out_shape=jax.ShapeDtypeStruct((rows, rhs),...  2.12 us

profile of v4, /device:TPU:0, one launch (start us, length us, event | category | flops | bytes accessed | tf_op | source)
XLA Modules:
  0.0 48.4 jit_solution(15828440608301150993)
XLA Ops:
  0.0 46.3 %coefficients.1 = (f32[2048,512]{1,0:T(8,128)S(1)}, f32[2048,256]{1,0:T(8,128)S(1)}, f32[256,256]{1,0:T(8,128)S(1)}) custom-call(f32[2048,512]{1,0:T(8,128)} %rs_hbm.1, f32[2048,512]{1,0:T(8,128)} %inv_hbm.1, f32[2048,256]{1,0:T(8,128)} %vm_hbm.1, f32[2048,256]{1,0:T(8,128)} %ym_hbm.1, f32[2,512,512]{2,1,0:T(8,128)} %mid_cap.1, f32[2048,256]{1,0:T(8,128)} %vt_hbm.1, ...), custom_call_target="tpu_custom_call" | custom-call | tf_op jit(solution)/shard_map/coefficients/pallas_call | solution.py:360
  46.3 2.1 %finish.1 = f32[2048,512]{1,0:T(8,128)} custom-call(f32[2048,512]{1,0:T(8,128)S(1)} %get-tuple-element.8.field, f32[2048,256]{1,0:T(8,128)S(1)} %get-tuple-element.9.yt, f32[256,256]{1,0:T(8,128)S(1)} %get-tuple-element.10.coef), custom_call_target="tpu_custom_call" | custom-call | tf_op jit(solution)/shard_map/finish/pallas_call | solution.py:416

commit v5 on v4

--- a/solution.py
+++ b/solution.py
@@ -57,9 +57,9 @@
 def coef_kernel(
     n, leaf, rank,
     rs_hbm, inv_hbm, vm_hbm, ym_hbm, mid_cap, vt_hbm, yt_hbm, top_cap,
-    field, yt, coef_last,
-    rs, inv, vm, vt, ym, cap, tcap,
-    inv3, v3, cap2, tcap2, d2,
+    field, basis, coef_last,
+    rs, inv, vm, vt, cap, tcap,
+    inv3, v3, cap2, tcap2, d2, factor3,
     proj, part, part_in, chip_sum, chip_in, pair, top_p, coef,
     d_part, d_part_in, d_sum, d_in, d_full,
     load_sem, cap_sem, send_sem, recv_sem,
@@ -87,8 +87,11 @@
     def ds(start, size):
         return pl.ds(pl.multiple_of(start, 8), size)
 
+    def columns(g):
+        return pl.ds(pl.multiple_of(g * cols, cols), cols)
+
     loads = (
-        (ym_hbm, ym), (vt_hbm, vt), (inv_hbm, inv), (vm_hbm, vm), (yt_hbm, yt), (rs_hbm, rs)
+        (ym_hbm, basis.at[0]), (vt_hbm, vt), (inv_hbm, inv), (vm_hbm, vm), (yt_hbm, basis.at[1])
     )
 
     def load(k, b):
@@ -97,7 +100,7 @@
         return pltpu.make_async_copy(src.at[at], dst.at[at], load_sem.at[k, b])
 
     def load_rs(g, b):
-        at = (ds(b * leaf, leaf), pl.ds(g * cols, cols))
+        at = (ds(b * leaf, leaf), columns(g))
         return pltpu.make_async_copy(rs_hbm.at[at], rs.at[at], load_sem.at[5 + g, b])
 
     def load_caps():
@@ -126,10 +129,16 @@
     for peer in peers:
         pl.semaphore_signal(barrier, inc=1, device_id=(peer,), device_id_type=MESH)
 
-    places = {}
-
-    def remote(key, src, dst, device):
-        at = places.setdefault(key, len(places))
+    sizes = dict(
+        a=GROUPS, b=GROUPS * chips, c=GROUPS, x=GROUPS, g=GROUPS * 2 * chips, f=GROUPS * 2,
+        da=1, db=chips, dz=1, dg=chips, df=1,
+    )
+    bases = {}
+    for kind, size in sizes.items():
+        bases[kind] = sum(sizes[k] for k in bases)
+
+    def remote(kind, sub, src, dst, device):
+        at = bases[kind] + sub
         return pltpu.make_async_remote_copy(
             src_ref=src, dst_ref=dst, send_sem=send_sem.at[at], recv_sem=recv_sem.at[at],
             device_id=(device,), device_id_type=MESH,
@@ -137,32 +146,32 @@
 
     others = tuple(reversed(range(1, chips)))
 
-    def spread(key, view):
-        return [remote((key, d), view, view, on_chip(d)) for d in others]
-
-    def same(key, view, device):
-        return [remote(key, view, view, device)]
+    def spread(kind, sub, view):
+        return [remote(kind, sub * chips + d, view, view, on_chip(d)) for d in others]
+
+    def same(kind, sub, view, device):
+        return [remote(kind, sub, view, view, device)]
 
     def d_own():
         return ds((core * chips + chip) * wd, wd)
 
     def d_core():
-        return [remote("da", d_part.at[ds((1 - core) * hd, hd)], d_part_in, partner)]
+        return [remote("da", 0, d_part.at[ds((1 - core) * hd, hd)], d_part_in, partner)]
 
     def d_chips():
         return [
-            remote(("db", d), d_sum.at[ds(flip(chip, d) * wd, wd)], d_in.at[d], on_chip(d))
+            remote("db", d, d_sum.at[ds(flip(chip, d) * wd, wd)], d_in.at[d], on_chip(d))
             for d in others
         ]
 
     def d_sibling():
-        return same("dz", d_full.at[side, d_own()], sibling)
+        return same("dz", 0, d_full.at[side, d_own()], sibling)
 
     def d_gather():
-        return spread("dg", d_full.at[:, d_own()])
+        return spread("dg", 0, d_full.at[:, d_own()])
 
     def d_forward():
-        return same("df", d_full.at[:, ds(core * hd, hd)], partner)
+        return same("df", 0, d_full.at[:, ds(core * hd, hd)], partner)
 
     def d_one():
         wait(d_core())
@@ -190,31 +199,31 @@
         d2[...] = both_parts(jnp.concatenate([d_full[0], d_full[1]], axis=1))
 
     def to_core(g):
-        return [remote(("a", g), part.at[g, ds((1 - core) * hr, hr)], part_in.at[g], partner)]
+        return [remote("a", g, part.at[g, ds((1 - core) * hr, hr)], part_in.at[g], partner)]
 
     def to_chips(g):
         return [
             remote(
-                ("b", g, d), chip_sum.at[g, ds(flip(chip, d) * w, w)], chip_in.at[g, d], on_chip(d)
+                "b", g * chips + d,
+                chip_sum.at[g, ds(flip(chip, d) * w, w)], chip_in.at[g, d], on_chip(d),
             )
             for d in others
         ]
 
     def to_sibling(g):
-        return same(("c", g), pair.at[g, side], sibling)
+        return same("c", g, pair.at[g, side], sibling)
 
     def to_across(g):
-        return same(("x", g), top_p.at[g, half], across)
+        return same("x", g, top_p.at[g, half], across)
 
     def own(g):
         return ds(g * cols + (core * chips + chip) * w, w)
 
     def gather(g, level):
-        return spread(("g", g, level), coef.at[own(g), pl.ds(level * rank, rank)])
+        return spread("g", g * 2 + level, coef.at[level, own(g)])
 
     def forward(g, level):
-        view = coef.at[ds(g * cols + core * hr, hr), pl.ds(level * rank, rank)]
-        return same(("f", g, level), view, partner)
+        return same("f", g * 2 + level, coef.at[level, ds(g * cols + core * hr, hr)], partner)
 
     def add_core(g):
         wait(to_core(g))
@@ -233,7 +242,7 @@
         wait(to_sibling(g))
         stacked = jnp.concatenate([pair[g, 1, :, :rank], pair[g, 0, :, :rank]], axis=1)
         both = small_dot(stacked, cap2, NT)
-        coef[own(g), :rank] = jnp.where(side == 0, both[:, :rank], both[:, rank:])
+        coef[0, own(g), :] = jnp.where(side == 0, both[:, :rank], both[:, rank:])
         return both
 
     def cross(g, both):
@@ -244,49 +253,28 @@
     def top(g):
         wait(to_across(g))
         stacked = jnp.concatenate([top_p[g, 1], top_p[g, 0]], axis=1)
-        coef[own(g), rank:] = small_dot(stacked, tcap2, NT)
+        coef[1, own(g), :] = small_dot(stacked, tcap2, NT)
         start(gather(g, 1))
 
     def pass_on(g, level):
         wait(gather(g, level))
         start(forward(g, level))
 
-    def correct_group(g, level):
+    def correct_task(task):
+        g, level = task // 2, task % 2
         wait(forward(g, level))
-        here = slice(g * cols, (g + 1) * cols)
-        factor = right3(coef[here, level * rank : (level + 1) * rank], 1)
-        basis = (ym, yt)[level]
+        here = columns(g)
+        factor3[...] = right3(coef[level, here_rows(g), :], 1)
 
         def step(b, _):
             at = ds(b * leaf, leaf)
-            field[at, here] -= dot(left3(basis[at, :]), factor, NT)
+            field[at, here] -= dot(left3(basis[level, at, :]), factor3[...], NT)
             return 0
 
         lax.fori_loop(0, blocks, step, 0)
 
-    def leaf_run(g, hooks):
-        here = slice(g * cols, (g + 1) * cols)
-
-        def step(i, _):
-            for when, hook in hooks:
-                pl.when(i == when)(hook)
-            outs = []
-            for b in (2 * i, 2 * i + 1):
-                at = ds(b * leaf, leaf)
-                if g == 0:
-                    wait([load(2, b), load(3, b)])
-                    inv3[at, :] = left3(inv[at, :])
-                    v3[b, :rank, :] = left3(vm[at, :].T)
-                wait([load_rs(g, b)])
-                out = dot(inv3[at, :], right3(rs[at, here], 0), NN)
-                field[at, here] = out
-                outs.append(right3(out, 0))
-            proj[...] += dot(v3[2 * i], outs[0], NN) + dot(v3[2 * i + 1], outs[1], NN)
-            return 0
-
-        proj[...] = jnp.zeros_like(proj)
-        lax.fori_loop(0, blocks // 2, step, 0)
-        part[g] = proj[...].T
+    def here_rows(g):
+        return ds(g * cols, cols)
 
     def split_caps():
         wait(load_caps())
@@ -300,46 +288,82 @@
         wait([load(0, b), load(1, b)])
         v = left3(vt[at, :].T)
         v3[b, rank:, :] = v
-        d_part[...] += dot(v, right3(ym[at, :], 0), NN)
+        d_part[...] += dot(v, right3(basis[0, at, :], 0), NN)
         return 0
 
     lax.fori_loop(0, blocks, d_step, 0)
     pl.semaphore_wait(barrier, len(peers))
     start(d_core())
-    leaf_run(0, ((1, d_one),))
-    start(to_core(0))
-    d_two()
-    split_caps()
-
-    def between():
-        add_core(0)
-        d_three()
-
-    leaf_run(1, ((1, between),))
-    start(to_core(1))
+
+    hooks = (
+        (1, d_one),
+        (blocks - 1, d_two),
+        (blocks, d_three),
+        (blocks + 1, lambda: add_core(0)),
+        (blocks + 2, d_four),
+        (blocks + 2, split_caps),
+    )
+
+    def leaf_step(i, _):
+        for when, hook in hooks:
+            pl.when(i == when)(hook)
+        g, b = i // blocks, i % blocks
+        at = ds(b * leaf, leaf)
+        wait([load_rs(g, b)])
+
+        @pl.when(g == 0)
+        def _():
+            wait([load(2, b), load(3, b)])
+            inv3[at, :] = left3(inv[at, :])
+            v3[b, :rank, :] = left3(vm[at, :].T)
+
+        @pl.when(b == 0)
+        def _():
+            proj[...] = jnp.zeros_like(proj)
+
+        out = dot(inv3[at, :], right3(rs[at, columns(g)], 0), NN)
+        field[at, columns(g)] = out
+        proj[...] += dot(v3[b], right3(out, 0), NN)
+
+        @pl.when(b == blocks - 1)
+        def _():
+            part[g] = proj[...].T
+            start(to_core(g))
+
+        return 0
+
+    lax.fori_loop(0, GROUPS * blocks, leaf_step, 0)
     add_chips(0)
-    d_four()
     add_core(1)
-    both = middle(0)
-    start(gather(0, 0))
     d_five()
-    cross(0, both)
-    add_chips(1)
-    top(0)
-    pass_on(0, 0)
-    both = middle(1)
-    cross(1, both)
-    start(gather(1, 0))
     wait([load(4, b) for b in range(blocks)])
-    correct_group(0, 0)
-    top(1)
+
+    def level_step(g, _):
+        both = middle(g)
+        start(gather(g, 0))
+        cross(g, both)
+        pl.when(g == 0)(lambda: add_chips(1))
+
+        @pl.when(g == 1)
+        def _():
+            pass_on(0, 0)
+            correct_task(0)
+
+        top(g)
+        return 0
+
+    lax.fori_loop(0, GROUPS, level_step, 0)
     pass_on(0, 1)
     pass_on(1, 0)
-    correct_group(0, 1)
-    pass_on(1, 1)
-    correct_group(1, 0)
+
+    def last_step(task, _):
+        pl.when(task == 2)(lambda: pass_on(1, 1))
+        correct_task(task)
+        return 0
+
+    lax.fori_loop(1, 3, last_step, 0)
     wait(forward(1, 1))
-    coef_last[...] = coef[cols:, rank:]
+    coef_last[...] = coef[1, cols:, :]
 
 
 def coefficients(n, rs, inv, vm, ym, mid_cap, vt, yt, top_cap):
@@ -352,25 +376,25 @@
     w, wd = cols // m, rank // m
     blocks = rows // leaf
     f32, bf16 = jnp.float32, jnp.bfloat16
-    copies = 2 * chips + 2 + GROUPS * (3 * chips + 2)
+    copies = 2 * chips + 3 + GROUPS * (3 * chips + 5)
 
     def vmem(*shape, dtype=f32):
         return pltpu.VMEM(shape, dtype)
 
     return pl.pallas_call(
         functools.partial(coef_kernel, n, leaf, rank),
-        out_shape=(vmem(rows, rhs), vmem(rows, rank), vmem(cols, rank)),
+        out_shape=(vmem(rows, rhs), vmem(2, rows, rank), vmem(cols, rank)),
         in_specs=[pl.BlockSpec(memory_space=pltpu.HBM)] * 8,
         out_specs=[pl.BlockSpec(memory_space=pltpu.VMEM)] * 3,
         scratch_shapes=[
             vmem(rows, rhs), vmem(rows, leaf), vmem(rows, rank), vmem(rows, rank),
-            vmem(rows, rank), vmem(2 * rank, 2 * rank), vmem(rank, 2 * rank),
+            vmem(2 * rank, 2 * rank), vmem(rank, 2 * rank),
             vmem(rows, 3 * leaf, dtype=bf16), vmem(blocks, 2 * rank, 3 * leaf, dtype=bf16),
             vmem(2, 2 * rank, 2 * rank, dtype=bf16), vmem(2, rank, 2 * rank, dtype=bf16),
-            vmem(2, rank, 2 * rank, dtype=bf16), vmem(2 * rank, cols),
+            vmem(2, rank, 2 * rank, dtype=bf16), vmem(cols, 3 * rank, dtype=bf16), vmem(2 * rank, cols),
             vmem(GROUPS, cols, 2 * rank), vmem(GROUPS, cols // 2, 2 * rank),
             vmem(GROUPS, cols // 2, 2 * rank), vmem(GROUPS, chips, w, 2 * rank),
-            vmem(GROUPS, 2, w, 2 * rank), vmem(GROUPS, 2, w, rank), vmem(rhs, 2 * rank),
+            vmem(GROUPS, 2, w, 2 * rank), vmem(GROUPS, 2, w, rank), vmem(2, rhs, rank),
             vmem(rank, rank), vmem(rank // 2, rank), vmem(rank // 2, rank),
             vmem(chips, wd, rank), vmem(2, rank, rank),
             pltpu.SemaphoreType.DMA((5 + GROUPS, blocks)),
@@ -379,36 +403,38 @@
             pltpu.SemaphoreType.DMA((copies,)),
         ],
         compiler_params=pltpu.CompilerParams(
-            collective_id=0, has_side_effects=True, vmem_limit_bytes=56 * 2**20
+            collective_id=0, has_side_effects=True, vmem_limit_bytes=54 * 2**20
         ),
         name="coefficients",
     )(rs, inv, vm, ym, mid_cap, vt, yt, top_cap)
 
 
-def finish_kernel(field, yt, coef, out, last, sem):
+def finish_kernel(field, basis, coef, out, last, factor3, sem):
     rows, rhs = out.shape
     cols = coef.shape[0]
     done = rhs - cols
-    tile = rows // 4
+    tiles = sem.shape[0] - 1
+    tile = rows // tiles
     left = pltpu.make_async_copy(
-        field.at[:, pl.ds(0, done)], out.at[:, pl.ds(0, done)], sem.at[4]
+        field.at[:, pl.ds(0, done)], out.at[:, pl.ds(0, done)], sem.at[tiles]
     )
     left.start()
-    factor = right3(coef[...], 1)
-    copies = []
-    for i in range(4):
-        at = slice(i * tile, (i + 1) * tile)
-        last[at, :] = field[at, done:] - dot(left3(yt[at, :]), factor, NT)
-        copy = pltpu.make_async_copy(
-            last.at[pl.ds(i * tile, tile)],
-            out.at[pl.ds(i * tile, tile), pl.ds(done, cols)],
-            sem.at[i],
-        )
+    factor3[...] = right3(coef[...], 1)
+
+    def right(i):
+        at = pl.ds(pl.multiple_of(i * tile, tile), tile)
+        return at, pltpu.make_async_copy(last.at[at], out.at[at, pl.ds(done, cols)], sem.at[i])
+
+    def step(i, _):
+        at, copy = right(i)
+        last[at, :] = field[at, done:] - dot(left3(basis[1, at, :]), factor3[...], NT)
         copy.start()
-        copies.append(copy)
+        return 0
+
+    lax.fori_loop(0, tiles, step, 0)
     left.wait()
-    for copy in copies:
-        copy.wait()
+    for i in range(tiles):
+        right(i)[1].wait()
 
 
 def finish(field, yt, coef):
@@ -420,6 +446,7 @@
         out_specs=pl.BlockSpec(memory_space=pltpu.HBM),
         scratch_shapes=[
             pltpu.VMEM((rows, coef.shape[0]), jnp.float32),
+            pltpu.VMEM((coef.shape[0], 3 * coef.shape[1]), jnp.bfloat16),
             pltpu.SemaphoreType.DMA((5,)),
         ],
         compiler_params=pltpu.CompilerParams(vmem_limit_bytes=16 * 2**20),

time: 48.6 us -> 49.7 us (1.023)
  Pallas kernels: 48.4 us -> 49.5 us
    pallas_call x1, Pallas kernels: 46.3 us -> 47 us  [coefficients(): pl.pallas_call(functools.partial(coef_kernel, n, leaf, rank), out_shape=(...]
where the time goes in v5:
time: 49.7 us; the launch traced here: 49.5 us
  Pallas kernels  49.5 us (100%)
    pallas_call x1, Pallas kernels, coefficients(): pl.pallas_call(functools.partial(coef_kernel, n, leaf, rank), out_shape=(...  47 us
    pallas_call x1, Pallas kernels, finish(): pl.pallas_call(finish_kernel, out_shape=jax.ShapeDtypeStruct((rows, rhs),...  2.49 us

profile of v5, /device:TPU:0, one launch (start us, length us, event | category | flops | bytes accessed | tf_op | source)
XLA Modules:
  0.0 49.5 jit_solution(8662302028261565268)
XLA Ops:
  0.0 47.0 %coefficients.1 = (f32[2048,512]{1,0:T(8,128)S(1)}, f32[2,2048,256]{2,1,0:T(8,128)S(1)}, f32[256,256]{1,0:T(8,128)S(1)}) custom-call(f32[2048,512]{1,0:T(8,128)} %rs_hbm.1, f32[2048,512]{1,0:T(8,128)} %inv_hbm.1, f32[2048,256]{1,0:T(8,128)} %vm_hbm.1, f32[2048,256]{1,0:T(8,128)} %ym_hbm.1, f32[2,512,512]{2,1,0:T(8,128)} %mid_cap.1, f32[2048,256]{1,0:T(8,128)} %vt_hbm.1, ...), custom_call_target="tpu_custom_call" | custom-call | tf_op jit(solution)/shard_map/coefficients/pallas_call | solution.py:384
  47.0 2.5 %finish.1 = f32[2048,512]{1,0:T(8,128)} custom-call(f32[2048,512]{1,0:T(8,128)S(1)} %get-tuple-element.8.field, f32[2,2048,256]{2,1,0:T(8,128)S(1)} %get-tuple-element.9.basis, f32[256,256]{1,0:T(8,128)S(1)} %get-tuple-element.10.coef), custom_call_target="tpu_custom_call" | custom-call | tf_op jit(solution)/shard_map/finish/pallas_call | solution.py:442

commit v6 on v5

--- a/solution.py
+++ b/solution.py
@@ -57,10 +57,10 @@
 def coef_kernel(
     n, leaf, rank,
     rs_hbm, inv_hbm, vm_hbm, ym_hbm, mid_cap, vt_hbm, yt_hbm, top_cap,
-    field, basis, coef_last,
-    rs, inv, vm, vt, cap, tcap,
-    inv3, v3, cap2, tcap2, d2, factor3,
-    proj, part, part_in, chip_sum, chip_in, pair, top_p, coef,
+    field, yt, coef_top,
+    rs, inv, vm, vt, ym, cap, tcap,
+    field3, v3, cap2, tcap2, d2, factor3,
+    part, part_in, chip_sum, chip_in, pair, top_p, coef,
     d_part, d_part_in, d_sum, d_in, d_full,
     load_sem, cap_sem, send_sem, recv_sem,
 ):
@@ -87,21 +87,14 @@
     def ds(start, size):
         return pl.ds(pl.multiple_of(start, 8), size)
 
-    def columns(g):
-        return pl.ds(pl.multiple_of(g * cols, cols), cols)
-
     loads = (
-        (ym_hbm, basis.at[0]), (vt_hbm, vt), (inv_hbm, inv), (vm_hbm, vm), (yt_hbm, basis.at[1])
+        (ym_hbm, ym), (vt_hbm, vt), (inv_hbm, inv), (rs_hbm, rs), (vm_hbm, vm), (yt_hbm, yt)
     )
 
     def load(k, b):
         src, dst = loads[k]
         at = ds(b * leaf, leaf)
         return pltpu.make_async_copy(src.at[at], dst.at[at], load_sem.at[k, b])
-
-    def load_rs(g, b):
-        at = (ds(b * leaf, leaf), columns(g))
-        return pltpu.make_async_copy(rs_hbm.at[at], rs.at[at], load_sem.at[5 + g, b])
 
     def load_caps():
         return [
@@ -118,11 +111,9 @@
             copy.wait()
 
     start([load(k, b) for b in range(blocks) for k in (0, 1)])
-    for b in range(blocks):
-        start([load(2, b), load_rs(0, b), load(3, b)])
-    start([load_rs(1, b) for b in range(blocks)])
+    start([load(k, b) for b in range(blocks) for k in (2, 3, 4)])
     start(load_caps())
-    start([load(4, b) for b in range(blocks)])
+    start([load(5, b) for b in range(blocks)])
 
     barrier = pltpu.get_barrier_semaphore()
     peers = [partner, sibling, across] + [on_chip(d) for d in range(1, chips)]
@@ -196,7 +187,7 @@
 
     def d_five():
         wait(d_forward())
-        d2[...] = both_parts(jnp.concatenate([d_full[0], d_full[1]], axis=1))
+        d2[...] = both_parts(jnp.concatenate([d_full[0], d_full[1]], axis=0))
 
     def to_core(g):
         return [remote("a", g, part.at[g, ds((1 - core) * hr, hr)], part_in.at[g], partner)]
@@ -247,7 +238,7 @@
 
     def cross(g, both):
         total = pair[g, 0, :, rank:] + pair[g, 1, :, rank:]
-        top_p[g, half] = total - small_dot(both, d2, NT)
+        top_p[g, half] = total - small_dot(both, d2, NN)
         start(to_across(g))
 
     def top(g):
@@ -260,21 +251,31 @@
         wait(gather(g, level))
         start(forward(g, level))
 
-    def correct_task(task):
-        g, level = task // 2, task % 2
-        wait(forward(g, level))
-        here = columns(g)
-        factor3[...] = right3(coef[level, here_rows(g), :], 1)
-
-        def step(b, _):
-            at = ds(b * leaf, leaf)
-            field[at, here] -= dot(left3(basis[level, at, :]), factor3[...], NT)
+    def correct_mid():
+        factor3[...] = right3(coef[0], 1)
+
+        def step(i, _):
+            for b in (2 * i, 2 * i + 1):
+                at = ds(b * leaf, leaf)
+                field[at, :] -= dot(left3(ym[at, :]), factor3[...], NT)
             return 0
 
-        lax.fori_loop(0, blocks, step, 0)
-
-    def here_rows(g):
-        return ds(g * cols, cols)
+        lax.fori_loop(0, blocks // 2, step, 0)
+
+    def project(g, hooks):
+        part[g] = jnp.zeros_like(part[g])
+
+        def step(i, _):
+            for when, hook in hooks:
+                pl.when(i == when)(hook)
+            b, here = 2 * i, slice(g * cols, (g + 1) * cols)
+            part[g] += dot(field3[b, here, :], v3[b], NN) + dot(
+                field3[b + 1, here, :], v3[b + 1], NN
+            )
+            return 0
+
+        lax.fori_loop(0, blocks // 2, step, 0)
+        start(to_core(g))
 
     def split_caps():
         wait(load_caps())
@@ -286,84 +287,62 @@
     def d_step(b, _):
         at = ds(b * leaf, leaf)
         wait([load(0, b), load(1, b)])
-        v = left3(vt[at, :].T)
-        v3[b, rank:, :] = v
-        d_part[...] += dot(v, right3(basis[0, at, :], 0), NN)
+        v = right3(vt[at, :], 0)
+        v3[b, :, rank:] = v
+        d_part[...] += dot(left3(ym[at, :].T), v, NN)
         return 0
 
     lax.fori_loop(0, blocks, d_step, 0)
     pl.semaphore_wait(barrier, len(peers))
     start(d_core())
 
-    hooks = (
-        (1, d_one),
-        (blocks - 1, d_two),
-        (blocks, d_three),
-        (blocks + 1, lambda: add_core(0)),
-        (blocks + 2, d_four),
-        (blocks + 2, split_caps),
-    )
-
     def leaf_step(i, _):
-        for when, hook in hooks:
-            pl.when(i == when)(hook)
-        g, b = i // blocks, i % blocks
-        at = ds(b * leaf, leaf)
-        wait([load_rs(g, b)])
-
-        @pl.when(g == 0)
-        def _():
-            wait([load(2, b), load(3, b)])
-            inv3[at, :] = left3(inv[at, :])
-            v3[b, :rank, :] = left3(vm[at, :].T)
-
-        @pl.when(b == 0)
-        def _():
-            proj[...] = jnp.zeros_like(proj)
-
-        out = dot(inv3[at, :], right3(rs[at, columns(g)], 0), NN)
-        field[at, columns(g)] = out
-        proj[...] += dot(v3[b], right3(out, 0), NN)
-
-        @pl.when(b == blocks - 1)
-        def _():
-            part[g] = proj[...].T
-            start(to_core(g))
-
+        pl.when(i == 1)(d_one)
+        for b in (2 * i, 2 * i + 1):
+            at = ds(b * leaf, leaf)
+            wait([load(2, b), load(3, b), load(4, b)])
+            out = dot(left3(inv[at, :]), right3(rs[at, :], 0), NN)
+            field[at, :] = out
+            field3[b] = left3(out.T)
+            v3[b, :, :rank] = right3(vm[at, :], 0)
         return 0
 
-    lax.fori_loop(0, GROUPS * blocks, leaf_step, 0)
+    lax.fori_loop(0, blocks // 2, leaf_step, 0)
+    d_two()
+    project(0, ())
+    d_three()
+    project(1, ((1, lambda: add_core(0)),))
+    split_caps()
+    add_core(1)
+    d_four()
     add_chips(0)
-    add_core(1)
     d_five()
-    wait([load(4, b) for b in range(blocks)])
 
     def level_step(g, _):
         both = middle(g)
         start(gather(g, 0))
         cross(g, both)
-        pl.when(g == 0)(lambda: add_chips(1))
+
+        @pl.when(g == 0)
+        def _():
+            add_chips(1)
 
         @pl.when(g == 1)
         def _():
             pass_on(0, 0)
-            correct_task(0)
 
         top(g)
         return 0
 
     lax.fori_loop(0, GROUPS, level_step, 0)
+    pass_on(1, 0)
     pass_on(0, 1)
-    pass_on(1, 0)
-
-    def last_step(task, _):
-        pl.when(task == 2)(lambda: pass_on(1, 1))
-        correct_task(task)
-        return 0
-
-    lax.fori_loop(1, 3, last_step, 0)
-    wait(forward(1, 1))
-    coef_last[...] = coef[1, cols:, :]
+    wait(forward(0, 0) + forward(1, 0))
+    wait([load(5, b) for b in range(blocks)])
+    correct_mid()
+    pass_on(1, 1)
+    wait(forward(0, 1) + forward(1, 1))
+    coef_top[...] = coef[1]
 
 
 def coefficients(n, rs, inv, vm, ym, mid_cap, vt, yt, top_cap):
@@ -383,58 +362,44 @@
 
     return pl.pallas_call(
         functools.partial(coef_kernel, n, leaf, rank),
-        out_shape=(vmem(rows, rhs), vmem(2, rows, rank), vmem(cols, rank)),
+        out_shape=(vmem(rows, rhs), vmem(rows, rank), vmem(rhs, rank)),
         in_specs=[pl.BlockSpec(memory_space=pltpu.HBM)] * 8,
         out_specs=[pl.BlockSpec(memory_space=pltpu.VMEM)] * 3,
         scratch_shapes=[
             vmem(rows, rhs), vmem(rows, leaf), vmem(rows, rank), vmem(rows, rank),
-            vmem(2 * rank, 2 * rank), vmem(rank, 2 * rank),
-            vmem(rows, 3 * leaf, dtype=bf16), vmem(blocks, 2 * rank, 3 * leaf, dtype=bf16),
+            vmem(rows, rank), vmem(2 * rank, 2 * rank), vmem(rank, 2 * rank),
+            vmem(blocks, rhs, 3 * leaf, dtype=bf16), vmem(blocks, 3 * leaf, 2 * rank, dtype=bf16),
             vmem(2, 2 * rank, 2 * rank, dtype=bf16), vmem(2, rank, 2 * rank, dtype=bf16),
-            vmem(2, rank, 2 * rank, dtype=bf16), vmem(cols, 3 * rank, dtype=bf16), vmem(2 * rank, cols),
+            vmem(2, 2 * rank, rank, dtype=bf16), vmem(rhs, 3 * rank, dtype=bf16),
             vmem(GROUPS, cols, 2 * rank), vmem(GROUPS, cols // 2, 2 * rank),
             vmem(GROUPS, cols // 2, 2 * rank), vmem(GROUPS, chips, w, 2 * rank),
             vmem(GROUPS, 2, w, 2 * rank), vmem(GROUPS, 2, w, rank), vmem(2, rhs, rank),
             vmem(rank, rank), vmem(rank // 2, rank), vmem(rank // 2, rank),
             vmem(chips, wd, rank), vmem(2, rank, rank),
-            pltpu.SemaphoreType.DMA((5 + GROUPS, blocks)),
+            pltpu.SemaphoreType.DMA((6, blocks)),
             pltpu.SemaphoreType.DMA((2,)),
             pltpu.SemaphoreType.DMA((copies,)),
             pltpu.SemaphoreType.DMA((copies,)),
         ],
         compiler_params=pltpu.CompilerParams(
-            collective_id=0, has_side_effects=True, vmem_limit_bytes=54 * 2**20
+            collective_id=0, has_side_effects=True, vmem_limit_bytes=55 * 2**20
         ),
         name="coefficients",
     )(rs, inv, vm, ym, mid_cap, vt, yt, top_cap)
 
 
-def finish_kernel(field, basis, coef, out, last, factor3, sem):
-    rows, rhs = out.shape
-    cols = coef.shape[0]
-    done = rhs - cols
-    tiles = sem.shape[0] - 1
-    tile = rows // tiles
-    left = pltpu.make_async_copy(
-        field.at[:, pl.ds(0, done)], out.at[:, pl.ds(0, done)], sem.at[tiles]
-    )
-    left.start()
-    factor3[...] = right3(coef[...], 1)
-
-    def right(i):
-        at = pl.ds(pl.multiple_of(i * tile, tile), tile)
-        return at, pltpu.make_async_copy(last.at[at], out.at[at, pl.ds(done, cols)], sem.at[i])
-
-    def step(i, _):
-        at, copy = right(i)
-        last[at, :] = field[at, done:] - dot(left3(basis[1, at, :]), factor3[...], NT)
-        copy.start()
-        return 0
-
-    lax.fori_loop(0, tiles, step, 0)
-    left.wait()
+def finish_kernel(field, yt, coef, out, last, sem):
+    tiles = sem.shape[0]
+    tile = out.shape[0] // tiles
+    factor = right3(coef[...], 1)
+    copies = []
     for i in range(tiles):
-        right(i)[1].wait()
+        at = pl.ds(i * tile, tile)
+        last[at, :] = field[at, :] - dot(left3(yt[at, :]), factor, NT)
+        copies.append(pltpu.make_async_copy(last.at[at], out.at[at], sem.at[i]))
+        copies[-1].start()
+    for copy in copies:
+        copy.wait()
 
 
 def finish(field, yt, coef):
@@ -445,11 +410,10 @@
         in_specs=[pl.BlockSpec(memory_space=pltpu.VMEM)] * 3,
         out_specs=pl.BlockSpec(memory_space=pltpu.HBM),
         scratch_shapes=[
-            pltpu.VMEM((rows, coef.shape[0]), jnp.float32),
-            pltpu.VMEM((coef.shape[0], 3 * coef.shape[1]), jnp.bfloat16),
-            pltpu.SemaphoreType.DMA((5,)),
+            pltpu.VMEM((rows, rhs), jnp.float32),
+            pltpu.SemaphoreType.DMA((4,)),
         ],
-        compiler_params=pltpu.CompilerParams(vmem_limit_bytes=16 * 2**20),
+        compiler_params=pltpu.CompilerParams(vmem_limit_bytes=24 * 2**20),
         name="finish",
     )(field, yt, coef)
 

time: 49.7 us -> 44.8 us (0.901)
  Pallas kernels: 49.5 us -> 44.7 us
    pallas_call x1, Pallas kernels: 47 us -> 41.8 us  [coefficients(): pl.pallas_call(functools.partial(coef_kernel, n, leaf, rank), out_shape=(...]
where the time goes in v6:
time: 44.8 us; the launch traced here: 44.7 us
  Pallas kernels  44.7 us (100%)
    pallas_call x1, Pallas kernels, coefficients(): pl.pallas_call(functools.partial(coef_kernel, n, leaf, rank), out_shape=(...  41.8 us
    pallas_call x1, Pallas kernels, finish(): pl.pallas_call(finish_kernel, out_shape=jax.ShapeDtypeStruct((rows, rhs),...  2.84 us

profile of v6, /device:TPU:0, one launch (start us, length us, event | category | flops | bytes accessed | tf_op | source)
XLA Modules:
  0.0 44.7 jit_solution(12340881307579790889)
XLA Ops:
  0.0 41.8 %coefficients.1 = (f32[2048,512]{1,0:T(8,128)S(1)}, f32[2048,256]{1,0:T(8,128)S(1)}, f32[512,256]{1,0:T(8,128)S(1)}) custom-call(f32[2048,512]{1,0:T(8,128)} %rs_hbm.1, f32[2048,512]{1,0:T(8,128)} %inv_hbm.1, f32[2048,256]{1,0:T(8,128)} %vm_hbm.1, f32[2048,256]{1,0:T(8,128)} %ym_hbm.1, f32[2,512,512]{2,1,0:T(8,128)} %mid_cap.1, f32[2048,256]{1,0:T(8,128)} %vt_hbm.1, ...), custom_call_target="tpu_custom_call" | custom-call | tf_op jit(solution)/shard_map/coefficients/pallas_call | solution.py:363
  41.9 2.8 %finish.1 = f32[2048,512]{1,0:T(8,128)} custom-call(f32[2048,512]{1,0:T(8,128)S(1)} %get-tuple-element.8.field, f32[2048,256]{1,0:T(8,128)S(1)} %get-tuple-element.9.yt, f32[512,256]{1,0:T(8,128)S(1)} %get-tuple-element.10.coef), custom_call_target="tpu_custom_call" | custom-call | tf_op jit(solution)/shard_map/finish/pallas_call | solution.py:407

commit v7 on v6

--- a/solution.py
+++ b/solution.py
@@ -296,45 +296,33 @@
     pl.semaphore_wait(barrier, len(peers))
     start(d_core())
 
-    def leaf_step(i, _):
-        pl.when(i == 1)(d_one)
-        for b in (2 * i, 2 * i + 1):
-            at = ds(b * leaf, leaf)
-            wait([load(2, b), load(3, b), load(4, b)])
-            out = dot(left3(inv[at, :]), right3(rs[at, :], 0), NN)
-            field[at, :] = out
-            field3[b] = left3(out.T)
-            v3[b, :, :rank] = right3(vm[at, :], 0)
-        return 0
-
-    lax.fori_loop(0, blocks // 2, leaf_step, 0)
-    d_two()
+    hooks = {1: d_one, blocks - 1: d_two}
+    for b in range(blocks):
+        hooks.get(b, lambda: None)()
+        at = slice(b * leaf, (b + 1) * leaf)
+        wait([load(2, b), load(3, b), load(4, b)])
+        out = dot(left3(inv[at, :]), right3(rs[at, :], 0), NN)
+        field[at, :] = out
+        field3[b] = left3(out.T)
+        v3[b, :, :rank] = right3(vm[at, :], 0)
+    d_three()
     project(0, ())
-    d_three()
+    d_four()
     project(1, ((1, lambda: add_core(0)),))
     split_caps()
     add_core(1)
-    d_four()
     add_chips(0)
     d_five()
-
-    def level_step(g, _):
-        both = middle(g)
-        start(gather(g, 0))
-        cross(g, both)
-
-        @pl.when(g == 0)
-        def _():
-            add_chips(1)
-
-        @pl.when(g == 1)
-        def _():
-            pass_on(0, 0)
-
-        top(g)
-        return 0
-
-    lax.fori_loop(0, GROUPS, level_step, 0)
+    both = middle(0)
+    cross(0, both)
+    add_chips(1)
+    start(gather(0, 0))
+    top(0)
+    both = middle(1)
+    start(gather(1, 0))
+    cross(1, both)
+    pass_on(0, 0)
+    top(1)
     pass_on(1, 0)
     pass_on(0, 1)
     wait(forward(0, 0) + forward(1, 0))

time: 44.8 us -> 44.8 us (level)
  no operation moved by 1% of the time
where the time goes in v7:
time: 44.8 us; the launch traced here: 44.7 us
  Pallas kernels  44.7 us (100%)
    pallas_call x1, Pallas kernels, coefficients(): pl.pallas_call(functools.partial(coef_kernel, n, leaf, rank), out_shape=(...  41.9 us
    pallas_call x1, Pallas kernels, finish(): pl.pallas_call(finish_kernel, out_shape=jax.ShapeDtypeStruct((rows, rhs),...  2.84 us

profile of v7, /device:TPU:0, one launch (start us, length us, event | category | flops | bytes accessed | tf_op | source)
XLA Modules:
  0.0 44.7 jit_solution(8814121405730071590)
XLA Ops:
  0.0 41.9 %coefficients.1 = (f32[2048,512]{1,0:T(8,128)S(1)}, f32[2048,256]{1,0:T(8,128)S(1)}, f32[512,256]{1,0:T(8,128)S(1)}) custom-call(f32[2048,512]{1,0:T(8,128)} %rs_hbm.1, f32[2048,512]{1,0:T(8,128)} %inv_hbm.1, f32[2048,256]{1,0:T(8,128)} %vm_hbm.1, f32[2048,256]{1,0:T(8,128)} %ym_hbm.1, f32[2,512,512]{2,1,0:T(8,128)} %mid_cap.1, f32[2048,256]{1,0:T(8,128)} %vt_hbm.1, ...), custom_call_target="tpu_custom_call" | custom-call | tf_op jit(solution)/shard_map/coefficients/pallas_call | solution.py:351
  41.9 2.8 %finish.1 = f32[2048,512]{1,0:T(8,128)} custom-call(f32[2048,512]{1,0:T(8,128)S(1)} %get-tuple-element.8.field, f32[2048,256]{1,0:T(8,128)S(1)} %get-tuple-element.9.yt, f32[512,256]{1,0:T(8,128)S(1)} %get-tuple-element.10.coef), custom_call_target="tpu_custom_call" | custom-call | tf_op jit(solution)/shard_map/finish/pallas_call | solution.py:395
